TPU v7x, 128 devices: a whole 4x4x4 slice. The times are simulated.
128 devices in a mesh: dp: 8 (over z_lo, x), mp: 16 (over y, z_hi, core).
Axes of the slice: x: 4, y: 4, z: 4 (z_hi: 2, z_lo: 2; z = z_hi * 2 + z_lo), core: 2. Of those that a mesh axis runs over, the one named last changes fastest.
Arguments:
- hidden_rows: bfloat16 [512, 16384], P('dp', 'mp'), may hold values from -60 to 60
- head_weight: bfloat16 [16384, 16, 8, 128], P('mp', None, 'dp'), may hold values from -0.046875 to 0.046875
- norm_gain: float32 [16, 8, 128], P('mp', 'dp'), may hold values from 0.1 to 1.9
- vocab_embed: bfloat16 [65536, 16, 8, 128], P('mp', None, 'dp'), may hold values from -6 to 6
- targets: int32 [512], replicated, may hold values from 0 to 65535
Outputs:
- weight_grad: bfloat16 [16384, 16, 8, 128], P('mp', None, 'dp')
- loss: float32 [], replicated
All inputs are finite; a program needn't handle non-finite values.
Results may differ from a plain program's by a relative error of at most 0.0046.
Values may be sent and summed in bfloat16 or wider, within the bound.
A program may use at most 128 MiB of HBM per device.

v0:
```python
import jax
import jax.numpy as jnp
from jax import lax
from jax.sharding import PartitionSpec as P


def on_device(hidden_rows, head_weight, norm_gain, vocab_embed, targets):
    tok_dp, width_mp = hidden_rows.shape
    n_mp = lax.axis_size("mp")
    block = head_weight.shape[3]
    width = width_mp * n_mp
    vocab_mp = vocab_embed.shape[0]
    dp_index = lax.axis_index("dp")
    mp_index = lax.axis_index("mp")
    contract = (((0,), (1,)), ((), ()))
    gathered = lax.all_gather(hidden_rows, "dp", axis=0, tiled=True)
    tokens_all = gathered.shape[0]
    weight_flat = head_weight.reshape(width_mp, n_mp * block)
    columns = weight_flat
    pre = lax.psum_scatter(
        lax.dot_general(columns, gathered, contract, preferred_element_type=jnp.float32),
        "mp",
        scatter_dimension=0,
        tiled=True,
    )
    own_rows = lax.dynamic_slice_in_dim(gathered, dp_index * block, block, 1).astype(jnp.float32).T
    act = own_rows + jax.nn.silu(pre)
    squares = lax.psum(jnp.sum(act * act, axis=0), ("dp", "mp"))
    inv = lax.rsqrt(squares / width + 1e-05)
    gain = norm_gain.reshape(block, 1)
    normed = (act * inv[None, :] * gain).astype(jnp.bfloat16)
    full_normed = lax.all_gather(normed, "mp", axis=0, tiled=True)
    embed_flat = vocab_embed.reshape(vocab_mp, n_mp * block)
    columns = full_normed
    logits = lax.psum_scatter(
        lax.dot_general(columns, embed_flat, contract, preferred_element_type=jnp.float32),
        "dp",
        scatter_dimension=0,
        tiled=True,
    )
    row_targets = lax.dynamic_slice_in_dim(targets, dp_index * tok_dp, tok_dp, 0)
    local_ids = row_targets - mp_index * vocab_mp
    hit = lax.broadcasted_iota(jnp.int32, logits.shape, 1) == local_ids[:, None]
    picked_here = jnp.sum(jnp.where(hit, logits, 0.0), axis=1)
    local_max = jnp.max(logits, axis=1)
    top = lax.pmax(local_max, "mp")
    total, picked = lax.psum((jnp.sum(jnp.exp(logits - top[:, None]), axis=1), picked_here), "mp")
    lse = top + jnp.log(total)
    dlogits = ((jnp.exp(logits - lse[:, None]) - hit.astype(jnp.float32)) / tokens_all).astype(
        jnp.bfloat16
    )
    loss = lax.psum(jnp.sum(lse - picked), "dp") / tokens_all
    all_dlogits = lax.all_gather(dlogits, "dp", axis=0, tiled=True)
    columns = embed_flat
    dnormed = lax.psum_scatter(
        lax.dot_general(columns, all_dlogits, contract, preferred_element_type=jnp.float32),
        "mp",
        scatter_dimension=0,
        tiled=True,
    )
    scaled = gain * dnormed
    inner = lax.psum(jnp.sum(act * scaled, axis=0), ("dp", "mp")) / width
    dact = inv[None, :] * scaled - act * (inv * inv * inv * inner)[None, :]
    sigma = jax.nn.sigmoid(pre)
    dpre = (dact * sigma * (1.0 + pre * (1.0 - sigma))).astype(jnp.bfloat16)
    all_dpre = lax.all_gather(dpre, "mp", axis=0, tiled=True)
    grad = lax.dot_general(
        gathered, all_dpre, (((0,), (1,)), ((), ())), preferred_element_type=jnp.float32
    )
    return (grad.astype(jnp.bfloat16).reshape(head_weight.shape), loss)


def solution(mesh):
    return jax.shard_map(
        on_device,
        mesh=mesh,
        in_specs=(
            P("dp", "mp"),
            P("mp", None, "dp", None),
            P("mp", "dp", None),
            P("mp", None, "dp", None),
            P(),
        ),
        out_specs=(P("mp", None, "dp", None), P()),
        check_vma=False,
    )
```

profile of v0, /device:TPU:1, one launch (start us, length us, event | category | flops | bytes accessed | tf_op | source)
XLA Modules:
  0.0 708.7 jit_solution(2290985431748103120)
XLA Ops:
  7.2 0.0 all-gather.5.cloned.1.call-start
  7.2 0.7 all-gather.5.cloned.1.call-update
  7.9 0.0 reduce-scatter.4.cloned.1.call-start
  7.9 38.8 %all-gather.5.cloned.1.call-done = bf16[512,1024]{1,0:T(8,128)(2,1)} async-done(((bf16[64,1024]{1,0:T(8,128)(2,1)}), bf16[512,1024]{1,0:T(8,128)(2,1)}) %all-gather.5.cloned.1.call-update) | async-done | bytes 1048592 | tf_op jit(solution)/shard_map/all_gather | solution.py:16
  46.8 7.0 fusion.6
  53.8 0.0 copy-start.1
  53.8 0.0 copy-start.2
  53.8 0.0 reduce-scatter.4.cloned.1.call-update
  53.8 0.0 all-gather.7.cloned.1.call-start
  53.9 1.1 copy-done.1
  55.0 0.1 copy.14
  55.2 81.9 %reduce-scatter.4.cloned.1.call-done = f32[128,512]{1,0:T(8,128)} async-done(((f32[2048,512]{1,0:T(8,128)}), f32[128,512]{1,0:T(8,128)}) %reduce-scatter.4.cloned.1.call-update) | async-done | bytes 262160 | tf_op jit(solution)/shard_map/reduce_scatter | solution.py:20
  137.1 1.1 multiply_reduce_fusion.1
  138.1 65.7 %psum.35 = f32[512]{0:T(512)S(1)} all-reduce(f32[512]{0:T(512)S(1)} %multiply_reduce_fusion.1), channel_id=1, replica_groups=mesh['dp'=8,'mp'=16] {'dp','mp'}, use_global_device_ids=true, to_apply=%region_2.3 | all-reduce | flops 512 | bytes 4096 | tf_op jit(solution)/shard_map/psum | solution.py:28
  203.9 0.0 copy-done.2
  203.9 1.7 multiply_convert_fusion.2
  205.6 0.0 all-gather.7.cloned.1.call-update
  205.6 0.0 reduce-scatter.6.cloned.1.call-start
  205.6 45.4 %all-gather.7.cloned.1.call-done = bf16[2048,512]{1,0:T(8,128)(2,1)} async-done(((bf16[128,512]{1,0:T(8,128)(2,1)}), bf16[2048,512]{1,0:T(8,128)(2,1)}) %all-gather.7.cloned.1.call-update) | async-done | bytes 2097168 | tf_op jit(solution)/shard_map/all_gather | solution.py:32
  251.0 15.2 %fusion.2 = f32[512,4096]{1,0:T(8,128)} fusion(bf16[2048,512]{1,0:T(8,128)(2,1)} %all-gather.7.cloned.1.call-done, bf16[512,8,16,128]{3,2,1,0:T(8,128)(2,1)} %bitcast.41), kind=kOutput, calls=%fused_computation.2 | convolution fusion | flops 8589934592 | bytes 27262976 | tf_op jit(solution)/shard_map/dot_general | solution.py:36
  266.3 0.0 reduce-scatter.6.cloned.1.call-update
  266.3 0.0 all-gather.9.cloned.1.call-start
  266.3 0.8 dynamic-slice_subtract_fusion
  267.1 90.3 %reduce-scatter.6.cloned.1.call-done = f32[64,4096]{1,0:T(8,128)} async-done(((f32[512,4096]{1,0:T(8,128)}), f32[64,4096]{1,0:T(8,128)}) %reduce-scatter.6.cloned.1.call-update) | async-done | bytes 1048592 | tf_op jit(solution)/shard_map/reduce_scatter | solution.py:35
  357.4 1.4 reduce_max.9
  358.8 33.2 %pmax.7 = f32[64]{0:T(128)S(1)} all-reduce(f32[64]{0:T(128)S(1)} %reduce_max.9), channel_id=1, replica_groups=mesh['dp'=8,'mp'=16] {'mp'}, use_global_device_ids=true, to_apply=%region_5.6 | all-reduce | flops 64 | bytes 512 | tf_op jit(solution)/shard_map/pmax | solution.py:46
  391.9 1.6 select_reduce_fusion
  393.6 37.7 %all-reduce = (f32[64]{0:T(128)S(1)}, f32[64]{0:T(128)S(1)}) all-reduce(f32[64]{0:T(128)S(1)} %get-tuple-element.7, f32[64]{0:T(128)S(1)} %get-tuple-element.6), channel_id=1, replica_groups=mesh['dp'=8,'mp'=16] {'mp'}, use_global_device_ids=true, to_apply=%region_7.8 | all-reduce | flops 128 | bytes 1024 | tf_op jit(solution)/shard_map/psum | solution.py:47
  431.2 0.6 subtract_reduce_fusion
  431.8 2.3 multiply_convert_fusion
  434.2 0.0 all-gather.9.cloned.1.call-update
  434.2 0.2 reduce-scatter.8.cloned.1.call-start
  434.4 46.6 %all-gather.9.cloned.1.call-done = bf16[512,4096]{1,0:T(8,128)(2,1)} async-done(((bf16[64,4096]{1,0:T(8,128)(2,1)}), bf16[512,4096]{1,0:T(8,128)(2,1)}) %all-gather.9.cloned.1.call-update) | async-done | bytes 4194320 | tf_op jit(solution)/shard_map/all_gather | solution.py:53
  481.1 15.0 %fusion.9 = f32[2048,512]{1,0:T(8,128)} fusion(bf16[512,4096]{1,0:T(8,128)(2,1)} %all-gather.9.cloned.1.call-done, bf16[512,8,16,128]{3,2,1,0:T(8,128)(2,1)} %bitcast.42), kind=kOutput, calls=%fused_computation.10 | convolution fusion | flops 8589934592 | bytes 25165824 | tf_op jit(solution)/shard_map/dot_general | solution.py:56
  496.1 0.0 copy-start
  496.1 0.0 reduce-scatter.8.cloned.1.call-update
  496.1 0.0 all-gather.11.cloned.1.call-start
  496.1 77.9 %reduce-scatter.8.cloned.1.call-done = f32[128,512]{1,0:T(8,128)} async-done(((f32[2048,512]{1,0:T(8,128)}), f32[128,512]{1,0:T(8,128)}) %reduce-scatter.8.cloned.1.call-update) | async-done | bytes 262160 | tf_op jit(solution)/shard_map/reduce_scatter | solution.py:55
  574.0 0.0 copy-done
  574.0 1.1 multiply_reduce_fusion
  575.1 65.7 %psum.37 = f32[512]{0:T(512)S(1)} all-reduce(f32[512]{0:T(512)S(1)} %multiply_reduce_fusion), channel_id=1, replica_groups=mesh['dp'=8,'mp'=16] {'dp','mp'}, use_global_device_ids=true, to_apply=%region_10.11 | all-reduce | flops 512 | bytes 4096 | tf_op jit(solution)/shard_map/psum | solution.py:62
  640.8 1.8 multiply_convert_fusion.1
  642.6 0.0 all-gather.11.cloned.1.call-update
  642.6 14.4 %psum.39 = f32[]{:T(128)} all-reduce(f32[]{:T(128)} %get-tuple-element.10), channel_id=1, replica_groups=mesh['dp'=8,'mp'=16] {'dp'}, use_global_device_ids=true, to_apply=%region_14.15 | all-reduce | flops 1 | bytes 8 | tf_op jit(solution)/shard_map/psum | solution.py:52
  657.7 30.4 %all-gather.11.cloned.1.call-done = bf16[2048,512]{1,0:T(8,128)(2,1)} async-done(((bf16[128,512]{1,0:T(8,128)(2,1)}), bf16[2048,512]{1,0:T(8,128)(2,1)}) %all-gather.11.cloned.1.call-update) | async-done | bytes 2097168 | tf_op jit(solution)/shard_map/all_gather | solution.py:66
  688.1 5.9 convolution_convert_fusion
  693.9 6.8 copy.12
  (3 shorter events, 0.0 us)
Async XLA Ops:
  7.2 39.6 %all-gather.5.cloned.1.call-start = ((), (), s32[]{:S(2)}) async-start(), calls=%async_computation.3 | async-start | bytes 1179648 | tf_op jit(solution)/shard_map/all_gather | solution.py:16
  7.9 129.2 %reduce-scatter.4.cloned.1.call-start = ((), (), s32[]{:S(2)}) async-start(), calls=%async_computation.4 | async-start | bytes 4456448 | tf_op jit(solution)/shard_map/reduce_scatter | solution.py:20
  53.8 1.2 copy-start.1
  53.8 150.1 %copy-start.2 = (f32[1,1,128]{2,1,0:T(1,128)S(1)}, f32[1,1,128]{2,1,0:T(1,128)}, u32[]{:S(2)}) copy-start(f32[1,1,128]{2,1,0:T(1,128)} %param.7) | copy-start | bytes 1540
  53.8 197.2 %all-gather.7.cloned.1.call-start = ((), (), s32[]{:S(2)}) async-start(), calls=%async_computation.5 | async-start | bytes 2228224 | tf_op jit(solution)/shard_map/all_gather | solution.py:32
  205.6 151.8 %reduce-scatter.6.cloned.1.call-start = ((), (), s32[]{:S(2)}) async-start(), calls=%async_computation.6 | async-start | bytes 9437184 | tf_op jit(solution)/shard_map/reduce_scatter | solution.py:35
  266.3 214.8 %all-gather.9.cloned.1.call-start = ((), (), s32[]{:S(2)}) async-start(), calls=%async_computation.7 | async-start | bytes 4718592 | tf_op jit(solution)/shard_map/all_gather | solution.py:53
  434.2 139.8 %reduce-scatter.8.cloned.1.call-start = ((), (), s32[]{:S(2)}) async-start(), calls=%async_computation.8 | async-start | bytes 4456448 | tf_op jit(solution)/shard_map/reduce_scatter | solution.py:55
  496.1 78.0 %copy-start = (f32[128,512]{1,0:T(8,128)S(1)}, f32[128,512]{1,0:T(8,128)}, u32[]{:S(2)}) copy-start(f32[128,512]{1,0:T(8,128)} %reduce-scatter.4.cloned.1.call-done) | copy-start | bytes 786436
  496.1 192.0 %all-gather.11.cloned.1.call-start = ((), (), s32[]{:S(2)}) async-start(), calls=%async_computation.9 | async-start | bytes 2228224 | tf_op jit(solution)/shard_map/all_gather | solution.py:66
Sparse Core Ops, SparseCore 0:
  9.6 37.0 all-gather.4
  53.9 83.1 reduce-scatter.3
  205.7 45.2 all-gather.6
  266.4 90.9 reduce-scatter.5
  434.3 46.6 all-gather.8
  496.2 77.7 reduce-scatter.7
  642.7 45.2 all-gather.10
where the time goes:
time: 709 us
  waiting for transfers between devices  412 us (58%)
  blocking collectives  217 us (31%)
  matrix products  43.1 us (6%)
  between operations  15.9 us (2%)
  other arithmetic  12.4 us (2%)
  local copies, waits for them, and re-layouts  8.1 us (1%)
    reduce_scatter x1, waiting for transfers between devices, on_device(): lax.psum_scatter(lax.dot_general(columns, embed_flat, contract, preferred...  90.3 us
    reduce_scatter x1, waiting for transfers between devices, on_device(): lax.psum_scatter(lax.dot_general(columns, gathered, contract, preferred_e...  81.9 us
    reduce_scatter x1, waiting for transfers between devices, on_device(): lax.psum_scatter(lax.dot_general(columns, all_dlogits, contract, preferre...  77.9 us
    psum x1, blocking collectives, on_device(): squares = lax.psum(jnp.sum(act * act, axis=0), ('dp', 'mp'))  65.7 us
    psum x1, blocking collectives, on_device(): inner = lax.psum(jnp.sum(act * scaled, axis=0), ('dp', 'mp')) / width  65.7 us
    all_gather x1, waiting for transfers between devices, on_device(): all_dlogits = lax.all_gather(dlogits, 'dp', axis=0, tiled=True)  46.6 us
    all_gather x1, waiting for transfers between devices, on_device(): full_normed = lax.all_gather(normed, 'mp', axis=0, tiled=True)  45.4 us
    all_gather x1, waiting for transfers between devices, on_device(): gathered = lax.all_gather(hidden_rows, 'dp', axis=0, tiled=True)  38.8 us
  transfers between devices with their start and end apart: 7, of which 7 were waited for; matrix products, arithmetic and copies ran while one was open for 0% of the time, Pallas kernels for 0%

commit v1 on v0

v1 whole, which is shorter than its diff:
```python
import jax
import jax.numpy as jnp
from jax import lax
from jax.experimental import pallas as pl
from jax.experimental.pallas import tpu as pltpu
from jax.sharding import PartitionSpec as P

MESH = pl.DeviceIdType.MESH
BF = jnp.bfloat16
F32 = jnp.float32
T, D, V, FB = 512, 16384, 4096, 128
CH = 1024
HALF = 512
NCH = V // CH
ROWS = 256
NT = (((1,), (1,)), ((), ()))
NN = (((1,), (0,)), ((), ()))


def dot(a, b, dims):
    return lax.dot_general(a, b, dims, preferred_element_type=F32)


def head_kernel(
    hid_ref, w_ref, gain_ref, e_ref, tgt_ref,
    dpf, hid_t, loss_ref,
    e_flat, w_flat, stage, hid_all, ps, core_in, ps2, mp_in, core_in2, mp_in2,
    pre_s, act_s, nb, nf, sq_own, sq_in, sq_sum, sq_in2, inv_s,
    lz, lx, rx, rz, sx2, rx2, sz2, rz2, lg, tsq, st_own, st_in, sc_all, dl,
    stage_sem, hid_ss, hid_rs, core_ss, core_rs, mp_ss, mp_rs, core2_ss, core2_rs, mp2_ss, mp2_rs,
    nf_ss, nf_rs, nfc_ss, nfc_rs, dp_ss, dp_rs, dpc_ss, dpc_rs,
    sq_ss, sq_rs, sq2_ss, sq2_rs, st_ss, st_rs, sc_ss, sc_rs,
    rx_ss, rx_rs, rz_ss, rz_rs, rx2_ss, rx2_rs, rz2_ss, rz2_rs,
    az_ss, az_rs, azz_ss, azz_rs, ax_ss, ax_rs, axf_ss, axf_rs, azf_ss, azf_rs, axz_ss, axz_rs,
):
    dp = lax.axis_index("dp")
    mp = lax.axis_index("mp")
    x, zl = lax.rem(dp, 4), dp // 4
    yz, c = mp // 2, lax.rem(mp, 2)
    y, zh = yz // 2, lax.rem(yz, 2)
    pos = x * 2 + zl

    def at_dp(dx, dz):
        return (lax.rem(zl + dz, 2) * 4 + lax.rem(x + dx, 4), mp)

    def at_mp(k, dc=0):
        return (dp, yz_of(k) * 2 + lax.rem(c + dc, 2))

    def yz_of(k):
        return lax.rem(y + k // 2, 4) * 2 + lax.rem(zh + k % 2, 2)

    def yz_from(k):
        return lax.rem(y + 4 - k // 2, 4) * 2 + lax.rem(zh + k % 2, 2)

    zpeer = at_dp(0, 1)
    sibling = at_mp(0, 1)
    dp_offs = [(k % 4, k // 4) for k in (6, 2, 5, 7, 1, 3, 4)]
    mp_offs = [5, 4, 3, 7, 2, 6, 1]
    mp15 = [(k, 1) for k in [*mp_offs, 0]] + [(k, 0) for k in mp_offs]

    def rc(src, dst, ss, rs, dev):
        return pltpu.make_async_remote_copy(
            src_ref=src, dst_ref=dst, send_sem=ss, recv_sem=rs, device_id=dev, device_id_type=MESH
        )

    def load_w(i):
        return pltpu.make_async_copy(w_ref.at[pl.ds(i * ROWS, ROWS)], stage.at[i], stage_sem.at[i])

    def load_e(i):
        slot = lax.rem(i, 4)
        return pltpu.make_async_copy(
            e_ref.at[pl.ds(i * ROWS, ROWS)], stage.at[slot], stage_sem.at[slot]
        )

    for i in range(4):
        load_w(i).start()

    barrier = pltpu.get_barrier_semaphore()
    for o in dp_offs:
        pl.semaphore_signal(barrier, inc=1, device_id=at_dp(*o), device_id_type=MESH)
    for k, dc in mp15:
        pl.semaphore_signal(barrier, inc=1, device_id=at_mp(k, dc), device_id_type=MESH)
    pl.semaphore_wait(barrier, len(dp_offs) + len(mp15))

    def send_hid(q):
        return rc(
            hid_ref, hid_all.at[pl.ds(pos * 64, 64)], hid_ss.at[q], hid_rs.at[q], at_dp(*dp_offs[q])
        )

    for q in range(7):
        send_hid(q).start()
    hid_all[pl.ds(pos * 64, 64), :] = hid_ref[...]

    def relay(slot, out, first):
        def body(i, carry):
            r = pltpu.einshape("vjl->jvl", stage[slot, pl.ds(pl.multiple_of(i * 64, 64), 64)])
            s = pl.multiple_of(first + i * 64, 64)
            for j in range(16):
                at = ((j % 2) * 8 + j // 2) * FB
                out[pl.ds(s, 64), at : at + FB] = r[j]
            return carry

        lax.fori_loop(0, ROWS // 64, body, 0)

    for i in range(4):
        load_w(i).wait()
        relay(i, w_flat, i * ROWS)
        load_e(i).start()

    for q in range(7):
        send_hid(q).wait_recv()

    def core_copy(buf, ss, rs, t):
        return rc(
            ps.at[1 - c, pl.ds(t * 2, 2)], buf.at[pl.ds(t * 2, 2)], ss.at[t], rs.at[t], sibling
        )

    def mp_copy(buf, ss, rs, k):
        return rc(ps2.at[yz_of(k)], buf.at[k], ss.at[k], rs.at[k], at_mp(k))

    def product(lhs, weight, cbuf, css, crs):
        for side in (1, 0):
            who = lax.rem(c + side, 2)

            def body(t, carry, who=who, side=side):
                col = pl.multiple_of(who * 1024 + t * 256, 256)
                r = dot(lhs[...], weight[:, pl.ds(col, 256)], NN).astype(BF)
                ps[who, t * 2] = r[:, :FB]
                ps[who, t * 2 + 1] = r[:, FB:]
                if side:
                    core_copy(cbuf, css, crs, t).start()
                return carry

            lax.fori_loop(0, 4, body, 0)

    def exchange(cbuf, css, crs, mbuf, mss, mrs):
        for t in range(4):
            core_copy(cbuf, css, crs, t).wait_recv()
        for k in [*mp_offs, 0]:
            b = yz_of(k)
            ps2[b] = (ps[c, b].astype(F32) + cbuf[b].astype(F32)).astype(BF)
            if k:
                mp_copy(mbuf, mss, mrs, k).start()

    def collect(cbuf, css, crs, mbuf, mss, mrs):
        total = ps[c, yz].astype(F32) + cbuf[yz].astype(F32)
        for k in mp_offs:
            mp_copy(mbuf, mss, mrs, k).wait_recv()
            total = total + mbuf[k].astype(F32)
        for k in mp_offs:
            mp_copy(mbuf, mss, mrs, k).wait_send()
        for t in range(4):
            core_copy(cbuf, css, crs, t).wait_send()
        return total

    product(hid_all, w_flat, core_in, core_ss, core_rs)
    exchange(core_in, core_ss, core_rs, mp_in, mp_ss, mp_rs)

    def relay_e(i, carry):
        load_e(i).wait()
        relay(lax.rem(i, 4), e_flat, i * ROWS)

        @pl.when(i + 4 < V // ROWS)
        def _():
            load_e(i + 4).start()

        return carry

    lax.fori_loop(0, V // ROWS, relay_e, 0)
    for i in range(8):
        hid_t[i * FB : (i + 1) * FB, :] = hid_all[:, i * FB : (i + 1) * FB].T

    pre = collect(core_in, core_ss, core_rs, mp_in, mp_ss, mp_rs)
    pre_s[...] = pre
    own = hid_all[:, pl.ds(pl.multiple_of(dp * FB, FB), FB)].astype(F32)
    act = own + pre / (1.0 + jnp.exp(-pre))
    act_s[...] = act
    gain = gain_ref[...]
    nb[...] = (act * gain).astype(BF)

    def cols(buf, core, b):
        return buf.at[:, pl.ds(pl.multiple_of((core * 8 + b) * FB, FB), FB)]

    def ag_copy(buf, ss, rs, k):
        return rc(nb, cols(buf, c, yz), ss.at[k], rs.at[k], at_mp(k))

    def ag_pass(buf, ss, rs, k):
        at = cols(buf, c, yz_from(k))
        return rc(nb if k == 0 else at, at, ss.at[k], rs.at[k], sibling)

    def gather_start(buf, ss, rs, css, crs):
        for k in mp_offs:
            ag_copy(buf, ss, rs, k).start()
        ag_pass(buf, css, crs, 0).start()
        buf[:, pl.ds(pl.multiple_of((c * 8 + yz) * FB, FB), FB)] = nb[...]

    def gather_end(buf, ss, rs, css, crs):
        for k in reversed(mp_offs):
            ag_copy(buf, ss, rs, k).wait_recv()
            ag_pass(buf, css, crs, k).start()
        for k in range(8):
            ag_pass(buf, css, crs, k).wait_recv()
        for k in range(8):
            ag_pass(buf, css, crs, k).wait_send()
        for k in mp_offs:
            ag_copy(buf, ss, rs, k).wait_send()

    gather_start(nf, nf_ss, nf_rs, nfc_ss, nfc_rs)

    def send_sq(q):
        k, dc = mp15[q]
        return rc(sq_own, sq_in.at[mp], sq_ss.at[q], sq_rs.at[q], at_mp(k, dc))

    squares = act * act
    for i in range(4):
        row = jnp.sum(squares[i * FB : (i + 1) * FB, :].T, axis=0, keepdims=True)
        sq_own[:, i * FB : (i + 1) * FB] = jnp.broadcast_to(row, (8, FB))
    for q in range(15):
        send_sq(q).start()
    sq_in[mp] = sq_own[...]

    gather_end(nf, nf_ss, nf_rs, nfc_ss, nfc_rs)

    def send_sq2(q):
        return rc(sq_sum, sq_in2.at[dp], sq2_ss.at[q], sq2_rs.at[q], at_dp(*dp_offs[q]))

    for q in range(15):
        send_sq(q).wait_recv()
    sq_sum[...] = jnp.sum(sq_in[...], axis=0)
    for q in range(7):
        send_sq2(q).start()
    sq_in2[dp] = sq_sum[...]

    def rows_of(xx, zz):
        return pl.ds(pl.multiple_of((xx * 2 + zz) * 64, 64), 64)

    def xd(d):
        return lax.rem(x + d, 4)

    def rz_copy(i, d):
        return rc(
            lz.at[i, rows_of(xd(d), 1 - zl)], rz.at[i, d], rz_ss.at[i, d], rz_rs.at[i, d], zpeer
        )

    def rx_copy(i, d):
        src = lx.at[i, pl.ds(pl.multiple_of(xd(d) * 128, 128), 128)]
        return rc(src, rx.at[i, d - 1], rx_ss.at[i, d - 1], rx_rs.at[i, d - 1], at_dp(d, 0))

    def rx2_copy(i):
        return rc(sx2.at[i], rx2.at[i], rx2_ss.at[i], rx2_rs.at[i], zpeer)

    def rz2_copy(i, d):
        return rc(
            sz2.at[i, d - 1], rz2.at[i, d - 1], rz2_ss.at[i, d - 1], rz2_rs.at[i, d - 1], at_dp(d, 0)
        )

    def zcol(i):
        return pl.ds(pl.multiple_of(i * CH, CH), HALF)

    def xcol(i):
        return pl.ds(pl.multiple_of(i * CH + HALF, HALF), HALF)

    def logits_chunk(i):
        at = pl.multiple_of(i * CH, CH)
        lz[i] = dot(nf[...], e_flat[pl.ds(at, HALF), :], NT).astype(BF)
        for d in (2, 1, 3, 0):
            rz_copy(i, d).start()
        lx[i] = dot(nf[...], e_flat[pl.ds(at + HALF, HALF), :], NT).astype(BF)
        for d in (2, 1, 3):
            rx_copy(i, d).start()

    def second_step(i):
        for d in (1, 3, 2):
            rx_copy(i, d).wait_recv()
        base = pl.multiple_of(x * 128, 128)
        for mine in (False, True):
            zz = zl if mine else 1 - zl
            off = pl.multiple_of(zz * 64, 64)
            s = lx[i, pl.ds(base + off, 64)].astype(F32)
            for d in range(3):
                s = s + rx[i, d, pl.ds(off, 64)].astype(F32)
            if mine:
                lg[:, xcol(i)] = s
            else:
                sx2[i] = s.astype(BF)
                rx2_copy(i).start()
        for d in (2, 1, 3, 0):
            rz_copy(i, d).wait_recv()
            s = lz[i, rows_of(xd(d), zl)].astype(F32) + rz[i, d].astype(F32)
            if d:
                sz2[i, d - 1] = s.astype(BF)
                rz2_copy(i, d).start()
            else:
                lg[:, zcol(i)] = s

    def rs_loop(i, carry):
        @pl.when(i < NCH)
        def _():
            logits_chunk(i)

        @pl.when(i > 0)
        def _():
            second_step(i - 1)

        return carry

    lax.fori_loop(0, NCH + 1, rs_loop, 0)

    for q in range(7):
        send_sq2(q).wait_recv()
    mean = jnp.sum(sq_in2[...], axis=0)[:1, :] / D
    inv_row = lax.rsqrt(mean + 1e-05)
    for i in range(4):
        part = jnp.broadcast_to(inv_row[:, i * FB : (i + 1) * FB], (FB, FB))
        inv_s[i * FB : (i + 1) * FB, :] = part.T

    def rs_end(i, carry):
        rx2_copy(i).wait_recv()
        lg[:, xcol(i)] = lg[:, xcol(i)] + rx2[i].astype(F32)
        s = lg[:, zcol(i)]
        for d in (1, 3, 2):
            rz2_copy(i, d).wait_recv()
            s = s + rz2[i, d - 1].astype(F32)
        lg[:, zcol(i)] = s
        return carry

    lax.fori_loop(0, NCH, rs_end, 0)

    my_rows = pl.ds(pl.multiple_of(pos * 64, 64), 64)
    inv_own = inv_s[my_rows, :][:, :1]
    lane = lax.broadcasted_iota(jnp.int32, (64, FB), 1)
    tgt = tgt_ref[...][:, :1]

    def scaled(i):
        at = pl.ds(pl.multiple_of(i * HALF, HALF), HALF)
        return lg[:, at], lax.broadcasted_iota(jnp.int32, (64, HALF), 1) + i * HALF

    def max_body(i, m):
        at = pl.ds(pl.multiple_of(i * HALF, HALF), HALF)
        v = lg[:, at] * inv_own
        lg[:, at] = v
        return jnp.maximum(m, jnp.max(v, axis=1, keepdims=True))

    m = lax.fori_loop(0, V // HALF, max_body, jnp.full((64, 1), -jnp.inf, F32))

    def sum_body(i, carry):
        s, sl, pk = carry
        v, ids = scaled(i)
        p = jnp.exp(v - m)
        s = s + jnp.sum(p, axis=1, keepdims=True)
        sl = sl + jnp.sum(p * v, axis=1, keepdims=True)
        pk = pk + jnp.sum(jnp.where(ids == tgt, v, 0.0), axis=1, keepdims=True)
        return s, sl, pk

    zero = jnp.zeros((64, 1), F32)
    s, sl, pk = lax.fori_loop(0, V // HALF, sum_body, (zero, zero, zero))
    tsq[...] = jnp.zeros((FB, FB), F32)
    tsq[:64, :] = jnp.where(
        lane == 0, m, jnp.where(lane == 1, s, jnp.where(lane == 2, sl, jnp.where(lane == 3, pk, 0.0)))
    )
    st_own[...] = tsq[...].T[:8, :]

    def send_st(q):
        k, dc = mp15[q]
        return rc(st_own, st_in.at[mp], st_ss.at[q], st_rs.at[q], at_mp(k, dc))

    for q in range(15):
        send_st(q).start()
    st_in[mp] = st_own[...]
    for q in range(15):
        send_st(q).wait_recv()
    all_m = st_in[:, 0, :]
    top = jnp.max(all_m, axis=0, keepdims=True)
    scale = jnp.exp(all_m - top)
    total = jnp.sum(st_in[:, 1, :] * scale, axis=0, keepdims=True)
    total_l = jnp.sum(st_in[:, 2, :] * scale, axis=0, keepdims=True)
    picked = jnp.sum(st_in[:, 3, :], axis=0, keepdims=True)
    valid = lax.broadcasted_iota(jnp.int32, (1, FB), 1) < 64
    total = jnp.where(valid, total, 1.0)
    lse = top + jnp.log(total)
    moment = (total_l / total - picked) / T
    sub = lax.broadcasted_iota(jnp.int32, (FB, FB), 0)
    table = jnp.where(sub == 0, lse, jnp.where(sub == 1, moment, jnp.where(sub == 2, lse - picked, 0.0)))
    tsq[...] = table.T
    sc_all[pos] = tsq[:64, :]

    def send_sc(q):
        return rc(sc_all.at[pos], sc_all.at[pos], sc_ss.at[q], sc_rs.at[q], at_dp(*dp_offs[q]))

    for q in range(7):
        send_sc(q).start()
    lse_col = tsq[:64, :][:, :1]

    def dl_at(xx, zz, col):
        return dl.at[rows_of(xx, zz), col]

    def az_copy(i, d):
        a = dl_at(x, zl, zcol(i))
        return rc(a, a, az_ss.at[i, d - 1], az_rs.at[i, d - 1], at_dp(d, 0))

    def azz_copy(i):
        a = dl_at(x, zl, zcol(i))
        return rc(a, a, azz_ss.at[i], azz_rs.at[i], zpeer)

    def azf_copy(i, d):
        a = dl_at(lax.rem(x + 4 - d, 4), zl, zcol(i))
        return rc(a, a, azf_ss.at[i, d - 1], azf_rs.at[i, d - 1], zpeer)

    def ax_copy(i, d):
        a = dl_at(x, zl, xcol(i))
        return rc(a, a, ax_ss.at[i, d - 1], ax_rs.at[i, d - 1], at_dp(d, 0))

    def axz_copy(i):
        a = dl_at(x, zl, xcol(i))
        return rc(a, a, axz_ss.at[i], axz_rs.at[i], zpeer)

    def axf_copy(i, d):
        a = dl_at(x, 1 - zl, xcol(i))
        return rc(a, a, axf_ss.at[i, d - 1], axf_rs.at[i, d - 1], at_dp(d, 0))

    def dl_body(i, carry):
        for h in (0, 1):
            v, ids = scaled(2 * i + h)
            p = jnp.exp(v - lse_col)
            at = pl.ds(pl.multiple_of(i * CH + h * HALF, HALF), HALF)
            dl[my_rows, at] = ((p - (ids == tgt).astype(F32)) / T).astype(BF)
            if h:
                axz_copy(i).start()
                for d in (2, 1, 3):
                    ax_copy(i, d).start()
            else:
                for d in (2, 1, 3):
                    az_copy(i, d).start()
                azz_copy(i).start()
        return carry

    lax.fori_loop(0, NCH, dl_body, 0)

    def fwd_body(i, carry):
        axz_copy(i).wait_recv()
        for d in (2, 1, 3):
            axf_copy(i, d).start()
        for d in (1, 3, 2):
            az_copy(i, d).wait_recv()
            azf_copy(i, d).start()
        return carry

    lax.fori_loop(0, NCH, fwd_body, 0)

    def ag_end(i, carry):
        azz_copy(i).wait_recv()
        for d in (1, 3, 2):
            ax_copy(i, d).wait_recv()
            axf_copy(i, d).wait_recv()
            azf_copy(i, d).wait_recv()
        return carry

    lax.fori_loop(0, NCH, ag_end, 0)

    product(dl, e_flat, core_in2, core2_ss, core2_rs)
    exchange(core_in2, core2_ss, core2_rs, mp_in2, mp2_ss, mp2_rs)
    for q in range(7):
        send_sc(q).wait_recv()
    loss = jnp.zeros((64, 1), F32)
    for b in range(8):
        loss = loss + sc_all[b][:, 2:3]
    loss_ref[...] = jnp.broadcast_to(jnp.sum(loss, axis=0, keepdims=True) / T, (8, FB))
    dnormed = collect(core_in2, core2_ss, core2_rs, mp_in2, mp2_ss, mp2_rs)
    moments = jnp.concatenate([sc_all[b][:, 1:2] for b in range(8)], axis=0)
    inv = inv_s[...]
    act = act_s[...]
    pre = pre_s[...]
    dact = inv * gain * dnormed - act * (inv * inv * (moments / D))
    sig = 1.0 / (1.0 + jnp.exp(-pre))
    nb[...] = (dact * sig * (1.0 + pre * (1.0 - sig))).astype(BF)
    gather_start(dpf, dp_ss, dp_rs, dpc_ss, dpc_rs)
    gather_end(dpf, dp_ss, dp_rs, dpc_ss, dpc_rs)

    for q in range(7):
        send_hid(q).wait_send()
        send_sq2(q).wait_send()
        send_sc(q).wait_send()
    for q in range(15):
        send_sq(q).wait_send()
        send_st(q).wait_send()

    def drain(i, carry):
        rx2_copy(i).wait_send()
        azz_copy(i).wait_send()
        axz_copy(i).wait_send()
        for d in range(4):
            rz_copy(i, d).wait_send()
        for d in (1, 2, 3):
            rx_copy(i, d).wait_send()
            rz2_copy(i, d).wait_send()
            az_copy(i, d).wait_send()
            azf_copy(i, d).wait_send()
            ax_copy(i, d).wait_send()
            axf_copy(i, d).wait_send()
        return carry

    lax.fori_loop(0, NCH, drain, 0)


def head(hidden, weight, gain, embed, tgt):
    vm = pltpu.VMEM
    dma = pltpu.SemaphoreType.DMA
    scratch = [
        vm((V, 2048), BF), vm((1024, 2048), BF), vm((4, ROWS, 16, FB), BF), vm((T, 1024), BF),
        vm((2, 8, T, FB), BF), vm((8, T, FB), BF), vm((8, T, FB), BF), vm((8, T, FB), BF),
        vm((8, T, FB), BF), vm((8, T, FB), BF),
        vm((T, FB), F32), vm((T, FB), F32), vm((T, FB), BF), vm((T, 2048), BF),
        vm((8, T), F32), vm((16, 8, T), F32), vm((8, T), F32), vm((8, 8, T), F32), vm((T, FB), F32),
        vm((NCH, T, HALF), BF), vm((NCH, T, HALF), BF),
        vm((NCH, 3, 128, HALF), BF), vm((NCH, 4, 64, HALF), BF),
        vm((NCH, 64, HALF), BF), vm((NCH, 64, HALF), BF), vm((NCH, 3, 64, HALF), BF), vm((NCH, 3, 64, HALF), BF),
        vm((64, V), F32), vm((FB, FB), F32), vm((8, FB), F32), vm((16, 8, FB), F32),
        vm((8, 64, FB), F32), vm((T, V), BF),
        dma((4,)),
    ]
    counts = [
        (7,), (4,), (8,), (4,), (8,), (8,), (8,), (8,), (8,), (15,), (7,), (15,), (7,),
        (NCH, 3), (NCH, 4), (NCH,), (NCH, 3),
        (NCH, 3), (NCH,), (NCH, 3), (NCH, 3), (NCH, 3), (NCH,),
    ]
    for n in counts:
        scratch += [dma(n), dma(n)]
    vspec = pl.BlockSpec(memory_space=pltpu.VMEM)
    anyspec = pl.BlockSpec(memory_space=pl.ANY)
    return pl.pallas_call(
        head_kernel,
        name="head",
        out_shape=(
            jax.ShapeDtypeStruct((T, 2048), BF),
            jax.ShapeDtypeStruct((1024, T), BF),
            jax.ShapeDtypeStruct((8, FB), F32),
        ),
        in_specs=[vspec, anyspec, vspec, anyspec, vspec],
        out_specs=(vspec, vspec, vspec),
        scratch_shapes=scratch,
        compiler_params=pltpu.CompilerParams(
            collective_id=0, has_side_effects=True, vmem_limit_bytes=62 << 20
        ),
    )(hidden, weight, gain, embed, tgt)


def grad_kernel(hid_t, dpf, out):
    r = dot(hid_t[...], dpf[...], NN).astype(BF)
    for j in range(16):
        at = ((j % 2) * 8 + j // 2) * FB
        out[:, j, :] = r[:, at : at + FB]


def weight_gradient(hid_t, dpf):
    rows = 128
    return pl.pallas_call(
        grad_kernel,
        name="weight_gradient",
        grid=(1024 // rows,),
        out_shape=jax.ShapeDtypeStruct((1024, 16, FB), BF),
        in_specs=[
            pl.BlockSpec((rows, T), lambda i: (i, 0)),
            pl.BlockSpec((T, 2048), lambda i: (0, 0)),
        ],
        out_specs=pl.BlockSpec((rows, 16, FB), lambda i: (i, 0, 0)),
        compiler_params=pltpu.CompilerParams(vmem_limit_bytes=32 << 20),
    )(hid_t, dpf)


def on_device(hidden_rows, head_weight, norm_gain, vocab_embed, targets):
    dp = lax.axis_index("dp")
    mp = lax.axis_index("mp")
    mine = lax.dynamic_slice_in_dim(targets, dp * 64, 64, 0) - mp * V
    dpf, hid_t, loss = head(
        hidden_rows,
        head_weight.reshape(1024, 16, FB),
        norm_gain.reshape(1, FB),
        vocab_embed.reshape(V, 16, FB),
        jnp.broadcast_to(mine[:, None], (64, FB)),
    )
    grad = weight_gradient(hid_t, dpf)
    return grad.reshape(head_weight.shape), loss[0, 0]


def solution(mesh):
    return jax.shard_map(
        on_device,
        mesh=mesh,
        in_specs=(
            P("dp", "mp"),
            P("mp", None, "dp", None),
            P("mp", "dp", None),
            P("mp", None, "dp", None),
            P(),
        ),
        out_specs=(P("mp", None, "dp", None), P()),
        check_vma=False,
    )
```

time: 709 us -> 209 us (0.29)
  waiting for transfers between devices: 412 us -> 0 us
  blocking collectives: 217 us -> 0 us
  Pallas kernels: 0 us -> 203 us
  matrix products: 43.1 us -> 0 us
  between operations: 15.9 us -> 0.65 us
  other arithmetic: 12.4 us -> 0.76 us
    reduce_scatter x3 -> x0, waiting for transfers between devices: 250 us -> none  [the longest x1 90.3 us: on_device(): lax.psum_scatter(lax.dot_general(columns, embed_flat, contract, preferred...]
    pallas_call x0 -> x2, Pallas kernels: none -> 203 us  [the longest x1 189 us: head(): pl.pallas_call(head_kernel, name='head', out_shape=(jax.ShapeDtypeStruct(...]
    psum x4 -> x0, blocking collectives: 183 us -> none  [the longest x1 65.7 us: on_device(): squares = lax.psum(jnp.sum(act * act, axis=0), ('dp', 'mp'))]
    all_gather x4 -> x0, waiting for transfers between devices: 161 us -> none  [the longest x1 46.6 us: on_device(): all_dlogits = lax.all_gather(dlogits, 'dp', axis=0, tiled=True)]
    dot_general x4 -> x0, matrix products: 43.1 us -> none  [the longest x1 15.2 us: on_device(): lax.dot_general(columns, embed_flat, contract, preferred_element_type=jnp...]
    pmax x1 -> x0, blocking collectives: 33.2 us -> none  [on_device(): top = lax.pmax(local_max, 'mp')]
  transfers between devices with their start and end apart: 7 -> 0, of which waited for: 7 -> 0; matrix products, arithmetic and copies ran while one was open for 0% -> 0% of each run, Pallas kernels for 0% -> 0%
where the time goes in v1:
time: 209 us
  Pallas kernels  203 us (97%)
  local copies, waits for them, and re-layouts  4.7 us (2%)
    pallas_call x1, Pallas kernels, head(): pl.pallas_call(head_kernel, name='head', out_shape=(jax.ShapeDtypeStruct(...  189 us
    pallas_call x1, Pallas kernels, weight_gradient(): pl.pallas_call(grad_kernel, name='weight_gradient', grid=(1024 // rows,),...  13.6 us

profile of v1, /device:TPU:1, one launch (start us, length us, event | category | flops | bytes accessed | tf_op | source)
XLA Modules:
  0.0 208.8 jit_solution(8506041550821223760)
XLA Ops:
  0.6 0.8 dynamic-slice_subtract_fusion
  1.4 0.7 broadcast_in_dim.2.tgt_ref
  2.1 189.1 %head.1 = (bf16[512,2048]{1,0:T(8,128)(2,1)}, bf16[1024,512]{1,0:T(8,128)(2,1)}, f32[8,128]{1,0:T(8,128)}) custom-call(bf16[64,1024]{1,0:T(8,128)(2,1)} %hid_ref.1, bf16[1024,16,128]{2,1,0:T(8,128)(2,1)} %bitcast.9, f32[1,128]{1,0:T(1,128)} %bitcast.10, bf16[4096,16,128]{2,1,0:T(8,128)(2,1)} %bitcast.7, s32[64,128]{1,0:T(8,128)} %broadcast_in_dim.2.tgt_ref), custom_call_target="tpu_custom_call" | custom-call | tf_op jit(solution)/shard_map/head/pallas_call | solution.py:530
  191.2 1.2 slice.3
  192.4 0.0 copy-start
  192.4 1.6 copy-done
  194.0 0.0 copy-start.1
  194.0 1.2 copy-done.1
  195.2 13.6 %weight_gradient.1 = bf16[1024,16,128]{2,1,0:T(8,128)(2,1)} custom-call(bf16[1024,512]{1,0:T(8,128)(2,1)S(1)} %copy-done.1, bf16[512,2048]{1,0:T(8,128)(2,1)S(1)} %copy-done), custom_call_target="tpu_custom_call" | custom-call | tf_op jit(solution)/shard_map/weight_gradient/pallas_call | solution.py:556
Async XLA Ops:
  192.4 1.6 copy-start
  194.0 1.2 copy-start.1

commit v2 on v1

--- a/solution.py
+++ b/solution.py
@@ -13,6 +13,9 @@
 HALF = 512
 NCH = V // CH
 ROWS = 256
+CODE = 32000.0
+PRE_BOUND = 60.0 * 0.046875 * 2048 * 1.01
+GRAD_BOUND = 6.0 * 2 / T * 1.01
 NT = (((1,), (1,)), ((), ()))
 NN = (((1,), (0,)), ((), ()))
 
@@ -22,9 +25,9 @@
 
 
 def head_kernel(
-    hid_ref, w_ref, gain_ref, e_ref, tgt_ref,
+    hid_ref, w_ref, gain_ref, e_ref, tgt_ref, all_tgt_ref,
     dpf, hid_t, loss_ref,
-    e_flat, w_flat, stage, hid_all, ps, core_in, ps2, mp_in, core_in2, mp_in2,
+    e_flat, w_flat, stage, hid_all, ps, acc, core_in, ps2, mp_in, oh, ct,
     pre_s, act_s, nb, nf, sq_own, sq_in, sq_sum, sq_in2, inv_s,
     lz, lx, rx, rz, sx2, rx2, sz2, rz2, lg, tsq, st_own, st_in, sc_all, dl,
     stage_sem, hid_ss, hid_rs, core_ss, core_rs, mp_ss, mp_rs, core2_ss, core2_rs, mp2_ss, mp2_rs,
@@ -110,51 +113,60 @@
     for q in range(7):
         send_hid(q).wait_recv()
 
-    def core_copy(buf, ss, rs, t):
-        return rc(
-            ps.at[1 - c, pl.ds(t * 2, 2)], buf.at[pl.ds(t * 2, 2)], ss.at[t], rs.at[t], sibling
-        )
-
-    def mp_copy(buf, ss, rs, k):
-        return rc(ps2.at[yz_of(k)], buf.at[k], ss.at[k], rs.at[k], at_mp(k))
-
-    def product(lhs, weight, cbuf, css, crs):
+    def core_copy(ss, rs, t):
+        return rc(ps.at[pl.ds(t * 2, 2)], core_in.at[pl.ds(t * 2, 2)], ss.at[t], rs.at[t], sibling)
+
+    def mp_copy(ss, rs, k):
+        return rc(ps2.at[yz_of(k)], mp_in.at[k], ss.at[k], rs.at[k], at_mp(k))
+
+    def product(tile, css, crs):
         for side in (1, 0):
             who = lax.rem(c + side, 2)
 
             def body(t, carry, who=who, side=side):
-                col = pl.multiple_of(who * 1024 + t * 256, 256)
-                r = dot(lhs[...], weight[:, pl.ds(col, 256)], NN).astype(BF)
-                ps[who, t * 2] = r[:, :FB]
-                ps[who, t * 2 + 1] = r[:, FB:]
+                first = who * 8 + t * 2
+                r = tile(first, pl.ds(pl.multiple_of(first * FB, 2 * FB), 2 * FB))
                 if side:
-                    core_copy(cbuf, css, crs, t).start()
+                    ps[t * 2] = r[:, :FB].astype(BF)
+                    ps[t * 2 + 1] = r[:, FB:].astype(BF)
+                    core_copy(css, crs, t).start()
+                else:
+                    acc[first] = r[:, :FB]
+                    acc[first + 1] = r[:, FB:]
                 return carry
 
             lax.fori_loop(0, 4, body, 0)
 
-    def exchange(cbuf, css, crs, mbuf, mss, mrs):
+    def encode(v, bound):
+        root = lax.rsqrt(lax.rsqrt(jnp.abs(v) * (CODE**4 / bound)))
+        code = (root + 0.5).astype(jnp.int32)
+        return jnp.where(v < 0, -code, code).astype(jnp.int16)
+
+    def decode(code, bound):
+        root = code.astype(F32) * (1.0 / CODE)
+        return root * jnp.abs(root) * (root * root) * bound
+
+    def exchange(css, crs, mss, mrs, bound):
         for t in range(4):
-            core_copy(cbuf, css, crs, t).wait_recv()
-        for k in [*mp_offs, 0]:
+            core_copy(css, crs, t).wait_recv()
+        for k in mp_offs:
             b = yz_of(k)
-            ps2[b] = (ps[c, b].astype(F32) + cbuf[b].astype(F32)).astype(BF)
-            if k:
-                mp_copy(mbuf, mss, mrs, k).start()
-
-    def collect(cbuf, css, crs, mbuf, mss, mrs):
-        total = ps[c, yz].astype(F32) + cbuf[yz].astype(F32)
+            ps2[b] = encode(acc[c * 8 + b] + core_in[b].astype(F32), bound)
+            mp_copy(mss, mrs, k).start()
+
+    def collect(css, crs, mss, mrs, bound):
+        total = acc[c * 8 + yz] + core_in[yz].astype(F32)
         for k in mp_offs:
-            mp_copy(mbuf, mss, mrs, k).wait_recv()
-            total = total + mbuf[k].astype(F32)
+            mp_copy(mss, mrs, k).wait_recv()
+            total = total + decode(mp_in[k], bound)
         for k in mp_offs:
-            mp_copy(mbuf, mss, mrs, k).wait_send()
+            mp_copy(mss, mrs, k).wait_send()
         for t in range(4):
-            core_copy(cbuf, css, crs, t).wait_send()
+            core_copy(css, crs, t).wait_send()
         return total
 
-    product(hid_all, w_flat, core_in, core_ss, core_rs)
-    exchange(core_in, core_ss, core_rs, mp_in, mp_ss, mp_rs)
+    product(lambda first, col: dot(hid_all[...], w_flat[:, col], NN), core_ss, core_rs)
+    exchange(core_ss, core_rs, mp_ss, mp_rs, PRE_BOUND)
 
     def relay_e(i, carry):
         load_e(i).wait()
@@ -170,7 +182,7 @@
     for i in range(8):
         hid_t[i * FB : (i + 1) * FB, :] = hid_all[:, i * FB : (i + 1) * FB].T
 
-    pre = collect(core_in, core_ss, core_rs, mp_in, mp_ss, mp_rs)
+    pre = collect(core_ss, core_rs, mp_ss, mp_rs, PRE_BOUND)
     pre_s[...] = pre
     own = hid_all[:, pl.ds(pl.multiple_of(dp * FB, FB), FB)].astype(F32)
     act = own + pre / (1.0 + jnp.exp(-pre))
@@ -218,6 +230,23 @@
     for q in range(15):
         send_sq(q).start()
     sq_in[mp] = sq_own[...]
+
+    all_tgt = all_tgt_ref[...][:, :1]
+    for i in range(NCH):
+        ids = lax.broadcasted_iota(jnp.int32, (T, HALF), 1) + i * CH
+        lz[i] = (ids == all_tgt).astype(BF)
+        lx[i] = (ids + HALF == all_tgt).astype(BF)
+
+    def pick_body(n, carry):
+        col = pl.ds(pl.multiple_of(n * 256, 256), 256)
+        r = jnp.zeros((T, 256), F32)
+        for i in range(NCH):
+            r = r + dot(lz[i], e_flat[i * CH : i * CH + HALF, col], NN)
+            r = r + dot(lx[i], e_flat[i * CH + HALF : (i + 1) * CH, col], NN)
+        oh[:, col] = r.astype(BF)
+        return carry
+
+    lax.fori_loop(0, 8, pick_body, 0)
 
     gather_end(nf, nf_ss, nf_rs, nfc_ss, nfc_rs)
 
@@ -326,14 +355,37 @@
 
     lax.fori_loop(0, NCH, rs_end, 0)
 
+    def dl_at(xx, zz, col):
+        return dl.at[rows_of(xx, zz), col]
+
+    def az_copy(i, d):
+        a = dl_at(x, zl, zcol(i))
+        return rc(a, a, az_ss.at[i, d - 1], az_rs.at[i, d - 1], at_dp(d, 0))
+
+    def azz_copy(i):
+        a = dl_at(x, zl, zcol(i))
+        return rc(a, a, azz_ss.at[i], azz_rs.at[i], zpeer)
+
+    def azf_copy(i, d):
+        a = dl_at(lax.rem(x + 4 - d, 4), zl, zcol(i))
+        return rc(a, a, azf_ss.at[i, d - 1], azf_rs.at[i, d - 1], zpeer)
+
+    def ax_copy(i, d):
+        a = dl_at(x, zl, xcol(i))
+        return rc(a, a, ax_ss.at[i, d - 1], ax_rs.at[i, d - 1], at_dp(d, 0))
+
+    def axz_copy(i):
+        a = dl_at(x, zl, xcol(i))
+        return rc(a, a, axz_ss.at[i], axz_rs.at[i], zpeer)
+
+    def axf_copy(i, d):
+        a = dl_at(x, 1 - zl, xcol(i))
+        return rc(a, a, axf_ss.at[i, d - 1], axf_rs.at[i, d - 1], at_dp(d, 0))
+
     my_rows = pl.ds(pl.multiple_of(pos * 64, 64), 64)
     inv_own = inv_s[my_rows, :][:, :1]
     lane = lax.broadcasted_iota(jnp.int32, (64, FB), 1)
     tgt = tgt_ref[...][:, :1]
-
-    def scaled(i):
-        at = pl.ds(pl.multiple_of(i * HALF, HALF), HALF)
-        return lg[:, at], lax.broadcasted_iota(jnp.int32, (64, HALF), 1) + i * HALF
 
     def max_body(i, m):
         at = pl.ds(pl.multiple_of(i * HALF, HALF), HALF)
@@ -343,17 +395,29 @@
 
     m = lax.fori_loop(0, V // HALF, max_body, jnp.full((64, 1), -jnp.inf, F32))
 
-    def sum_body(i, carry):
+    def exp_body(i, carry):
         s, sl, pk = carry
-        v, ids = scaled(i)
-        p = jnp.exp(v - m)
-        s = s + jnp.sum(p, axis=1, keepdims=True)
-        sl = sl + jnp.sum(p * v, axis=1, keepdims=True)
-        pk = pk + jnp.sum(jnp.where(ids == tgt, v, 0.0), axis=1, keepdims=True)
+        for h in (0, 1):
+            at = pl.ds(pl.multiple_of(i * CH + h * HALF, HALF), HALF)
+            ids = lax.broadcasted_iota(jnp.int32, (64, HALF), 1) + (i * CH + h * HALF)
+            v = lg[:, at]
+            p = jnp.exp(v - m)
+            dl[my_rows, at] = p.astype(BF)
+            if h:
+                axz_copy(i).start()
+                for d in (2, 1, 3):
+                    ax_copy(i, d).start()
+            else:
+                for d in (2, 1, 3):
+                    az_copy(i, d).start()
+                azz_copy(i).start()
+            s = s + jnp.sum(p, axis=1, keepdims=True)
+            sl = sl + jnp.sum(p * v, axis=1, keepdims=True)
+            pk = pk + jnp.sum(jnp.where(ids == tgt, v, 0.0), axis=1, keepdims=True)
         return s, sl, pk
 
     zero = jnp.zeros((64, 1), F32)
-    s, sl, pk = lax.fori_loop(0, V // HALF, sum_body, (zero, zero, zero))
+    s, sl, pk = lax.fori_loop(0, NCH, exp_body, (zero, zero, zero))
     tsq[...] = jnp.zeros((FB, FB), F32)
     tsq[:64, :] = jnp.where(
         lane == 0, m, jnp.where(lane == 1, s, jnp.where(lane == 2, sl, jnp.where(lane == 3, pk, 0.0)))
@@ -367,6 +431,18 @@
     for q in range(15):
         send_st(q).start()
     st_in[mp] = st_own[...]
+
+    def fwd_body(i, carry):
+        axz_copy(i).wait_recv()
+        for d in (2, 1, 3):
+            axf_copy(i, d).start()
+        for d in (1, 3, 2):
+            az_copy(i, d).wait_recv()
+            azf_copy(i, d).start()
+        return carry
+
+    lax.fori_loop(0, 2, fwd_body, 0)
+
     for q in range(15):
         send_st(q).wait_recv()
     all_m = st_in[:, 0, :]
@@ -379,8 +455,9 @@
     total = jnp.where(valid, total, 1.0)
     lse = top + jnp.log(total)
     moment = (total_l / total - picked) / T
+    factor = jnp.exp(st_own[:1, :] - lse) / T
     sub = lax.broadcasted_iota(jnp.int32, (FB, FB), 0)
-    table = jnp.where(sub == 0, lse, jnp.where(sub == 1, moment, jnp.where(sub == 2, lse - picked, 0.0)))
+    table = jnp.where(sub == 0, factor, jnp.where(sub == 1, moment, jnp.where(sub == 2, lse - picked, 0.0)))
     tsq[...] = table.T
     sc_all[pos] = tsq[:64, :]
 
@@ -389,83 +466,53 @@
 
     for q in range(7):
         send_sc(q).start()
-    lse_col = tsq[:64, :][:, :1]
-
-    def dl_at(xx, zz, col):
-        return dl.at[rows_of(xx, zz), col]
-
-    def az_copy(i, d):
-        a = dl_at(x, zl, zcol(i))
-        return rc(a, a, az_ss.at[i, d - 1], az_rs.at[i, d - 1], at_dp(d, 0))
-
-    def azz_copy(i):
-        a = dl_at(x, zl, zcol(i))
-        return rc(a, a, azz_ss.at[i], azz_rs.at[i], zpeer)
-
-    def azf_copy(i, d):
-        a = dl_at(lax.rem(x + 4 - d, 4), zl, zcol(i))
-        return rc(a, a, azf_ss.at[i, d - 1], azf_rs.at[i, d - 1], zpeer)
-
-    def ax_copy(i, d):
-        a = dl_at(x, zl, xcol(i))
-        return rc(a, a, ax_ss.at[i, d - 1], ax_rs.at[i, d - 1], at_dp(d, 0))
-
-    def axz_copy(i):
-        a = dl_at(x, zl, xcol(i))
-        return rc(a, a, axz_ss.at[i], axz_rs.at[i], zpeer)
-
-    def axf_copy(i, d):
-        a = dl_at(x, 1 - zl, xcol(i))
-        return rc(a, a, axf_ss.at[i, d - 1], axf_rs.at[i, d - 1], at_dp(d, 0))
-
-    def dl_body(i, carry):
-        for h in (0, 1):
-            v, ids = scaled(2 * i + h)
-            p = jnp.exp(v - lse_col)
-            at = pl.ds(pl.multiple_of(i * CH + h * HALF, HALF), HALF)
-            dl[my_rows, at] = ((p - (ids == tgt).astype(F32)) / T).astype(BF)
-            if h:
-                axz_copy(i).start()
-                for d in (2, 1, 3):
-                    ax_copy(i, d).start()
-            else:
-                for d in (2, 1, 3):
-                    az_copy(i, d).start()
-                azz_copy(i).start()
-        return carry
-
-    lax.fori_loop(0, NCH, dl_body, 0)
-
-    def fwd_body(i, carry):
-        axz_copy(i).wait_recv()
-        for d in (2, 1, 3):
-            axf_copy(i, d).start()
-        for d in (1, 3, 2):
-            az_copy(i, d).wait_recv()
-            azf_copy(i, d).start()
-        return carry
-
-    lax.fori_loop(0, NCH, fwd_body, 0)
-
-    def ag_end(i, carry):
+
+    lax.fori_loop(2, NCH, fwd_body, 0)
+
+    def ag_end(i):
         azz_copy(i).wait_recv()
         for d in (1, 3, 2):
             ax_copy(i, d).wait_recv()
             axf_copy(i, d).wait_recv()
             azf_copy(i, d).wait_recv()
-        return carry
-
-    lax.fori_loop(0, NCH, ag_end, 0)
-
-    product(dl, e_flat, core_in2, core2_ss, core2_rs)
-    exchange(core_in2, core2_ss, core2_rs, mp_in2, mp2_ss, mp2_rs)
+
+    def part(i, col):
+        at = pl.multiple_of(i * CH, CH)
+        return dot(dl[:, pl.ds(at, CH)], e_flat[pl.ds(at, CH), col], NN)
+
+    for i in range(NCH - 1):
+        ag_end(i)
+
+        def part_body(t, carry, i=i):
+            r = part(i, pl.ds(pl.multiple_of(t * 256, 256), 256))
+            for h in (0, 1):
+                v = r[:, h * FB : (h + 1) * FB]
+                acc[t * 2 + h] = v if i == 0 else acc[t * 2 + h] + v
+            return carry
+
+        lax.fori_loop(0, 8, part_body, 0)
+
     for q in range(7):
         send_sc(q).wait_recv()
     loss = jnp.zeros((64, 1), F32)
     for b in range(8):
         loss = loss + sc_all[b][:, 2:3]
+        ct[b * 64 : (b + 1) * 64, :] = jnp.broadcast_to(sc_all[b][:, 0:1], (64, FB))
     loss_ref[...] = jnp.broadcast_to(jnp.sum(loss, axis=0, keepdims=True) / T, (8, FB))
-    dnormed = collect(core_in2, core2_ss, core2_rs, mp_in2, mp2_ss, mp2_rs)
+    ag_end(NCH - 1)
+
+    def last_tile(first, col):
+        r = part(NCH - 1, col)
+        f = ct[...]
+        own_row = oh[:, col].astype(F32) / T
+        return jnp.concatenate(
+            [(acc[first + h] + r[:, h * FB : (h + 1) * FB]) * f - own_row[:, h * FB : (h + 1) * FB] for h in (0, 1)],
+            axis=1,
+        )
+
+    product(last_tile, core2_ss, core2_rs)
+    exchange(core2_ss, core2_rs, mp2_ss, mp2_rs, GRAD_BOUND)
+    dnormed = collect(core2_ss, core2_rs, mp2_ss, mp2_rs, GRAD_BOUND)
     moments = jnp.concatenate([sc_all[b][:, 1:2] for b in range(8)], axis=0)
     inv = inv_s[...]
     act = act_s[...]
@@ -502,13 +549,13 @@
     lax.fori_loop(0, NCH, drain, 0)
 
 
-def head(hidden, weight, gain, embed, tgt):
+def head(hidden, weight, gain, embed, tgt, all_tgt):
     vm = pltpu.VMEM
     dma = pltpu.SemaphoreType.DMA
     scratch = [
         vm((V, 2048), BF), vm((1024, 2048), BF), vm((4, ROWS, 16, FB), BF), vm((T, 1024), BF),
-        vm((2, 8, T, FB), BF), vm((8, T, FB), BF), vm((8, T, FB), BF), vm((8, T, FB), BF),
-        vm((8, T, FB), BF), vm((8, T, FB), BF),
+        vm((8, T, FB), BF), vm((16, T, FB), F32), vm((8, T, FB), BF), vm((8, T, FB), jnp.int16),
+        vm((8, T, FB), jnp.int16), vm((T, 2048), BF), vm((T, FB), F32),
         vm((T, FB), F32), vm((T, FB), F32), vm((T, FB), BF), vm((T, 2048), BF),
         vm((8, T), F32), vm((16, 8, T), F32), vm((8, T), F32), vm((8, 8, T), F32), vm((T, FB), F32),
         vm((NCH, T, HALF), BF), vm((NCH, T, HALF), BF),
@@ -535,20 +582,19 @@
             jax.ShapeDtypeStruct((1024, T), BF),
             jax.ShapeDtypeStruct((8, FB), F32),
         ),
-        in_specs=[vspec, anyspec, vspec, anyspec, vspec],
+        in_specs=[vspec, anyspec, vspec, anyspec, vspec, vspec],
         out_specs=(vspec, vspec, vspec),
         scratch_shapes=scratch,
         compiler_params=pltpu.CompilerParams(
             collective_id=0, has_side_effects=True, vmem_limit_bytes=62 << 20
         ),
-    )(hidden, weight, gain, embed, tgt)
+    )(hidden, weight, gain, embed, tgt, all_tgt)
 
 
 def grad_kernel(hid_t, dpf, out):
     r = dot(hid_t[...], dpf[...], NN).astype(BF)
-    for j in range(16):
-        at = ((j % 2) * 8 + j // 2) * FB
-        out[:, j, :] = r[:, at : at + FB]
+    blocks = jnp.stack([r[:, ((j % 2) * 8 + j // 2) * FB :][:, :FB] for j in range(16)])
+    out[...] = pltpu.einshape("jvl->vjl", blocks)
 
 
 def weight_gradient(hid_t, dpf):
@@ -570,13 +616,16 @@
 def on_device(hidden_rows, head_weight, norm_gain, vocab_embed, targets):
     dp = lax.axis_index("dp")
     mp = lax.axis_index("mp")
-    mine = lax.dynamic_slice_in_dim(targets, dp * 64, 64, 0) - mp * V
+    local = targets - mp * V
+    mine = lax.dynamic_slice_in_dim(local, dp * 64, 64, 0)
+    ordered = local.reshape(2, 4, 64).transpose(1, 0, 2).reshape(T)
     dpf, hid_t, loss = head(
         hidden_rows,
         head_weight.reshape(1024, 16, FB),
         norm_gain.reshape(1, FB),
         vocab_embed.reshape(V, 16, FB),
         jnp.broadcast_to(mine[:, None], (64, FB)),
+        jnp.broadcast_to(ordered[:, None], (T, FB)),
     )
     grad = weight_gradient(hid_t, dpf)
     return grad.reshape(head_weight.shape), loss[0, 0]

time: 209 us -> 193 us (0.923)
  Pallas kernels: 203 us -> 185 us
    pallas_call x1, Pallas kernels: 189 us -> 180 us  [head(): pl.pallas_call(head_kernel, name='head', out_shape=(jax.ShapeDtypeStruct(...]
    pallas_call x1, Pallas kernels: 13.6 us -> 5.52 us  [weight_gradient(): pl.pallas_call(grad_kernel, name='weight_gradient', grid=(1024 // rows,),...]
where the time goes in v2:
time: 193 us; the launch traced here: 192 us
  Pallas kernels  185 us (96%)
  local copies, waits for them, and re-layouts  5.76 us (3%)
    pallas_call x1, Pallas kernels, head(): pl.pallas_call(head_kernel, name='head', out_shape=(jax.ShapeDtypeStruct(...  180 us
    pallas_call x1, Pallas kernels, weight_gradient(): pl.pallas_call(grad_kernel, name='weight_gradient', grid=(1024 // rows,),...  5.52 us

profile of v2, /device:TPU:1, one launch (start us, length us, event | category | flops | bytes accessed | tf_op | source)
XLA Modules:
  0.0 192.5 jit_solution(5247567304964867437)
XLA Ops:
  0.6 0.7 broadcast_subtract_fusion
  1.3 0.1 dynamic_slice.3
  1.4 0.1 reshape.24
  1.5 0.1 broadcast_in_dim.14
  1.6 0.7 broadcast_in_dim.6.tgt_ref
  2.3 0.8 broadcast_in_dim.15.all_tgt_ref
  3.1 179.9 %head.1 = (bf16[512,2048]{1,0:T(8,128)(2,1)}, bf16[1024,512]{1,0:T(8,128)(2,1)}, f32[8,128]{1,0:T(8,128)}) custom-call(bf16[64,1024]{1,0:T(8,128)(2,1)} %hid_ref.1, bf16[1024,16,128]{2,1,0:T(8,128)(2,1)} %bitcast.10, f32[1,128]{1,0:T(1,128)} %bitcast.12, bf16[4096,16,128]{2,1,0:T(8,128)(2,1)} %bitcast.8, s32[64,128]{1,0:T(8,128)} %broadcast_in_dim.6.tgt_ref, ...), custom_call_target="tpu_custom_call" | custom-call | tf_op jit(solution)/shard_map/head/pallas_call | solution.py:577
  183.0 1.2 slice.3
  184.1 0.0 copy-start
  184.1 1.6 copy-done
  185.7 0.0 copy-start.1
  185.7 1.2 copy-done.1
  186.9 5.5 %weight_gradient.1 = bf16[1024,16,128]{2,1,0:T(8,128)(2,1)} custom-call(bf16[1024,512]{1,0:T(8,128)(2,1)S(1)} %copy-done.1, bf16[512,2048]{1,0:T(8,128)(2,1)S(1)} %copy-done), custom_call_target="tpu_custom_call" | custom-call | tf_op jit(solution)/shard_map/weight_gradient/pallas_call | solution.py:602
  (1 shorter events, 0.0 us)
Async XLA Ops:
  184.1 1.6 copy-start
  185.7 1.2 copy-start.1

commit v3 on v0

v3 whole, which is shorter than its diff:
```python
import jax
import jax.numpy as jnp
from jax import lax
from jax.experimental import pallas as pl
from jax.experimental.pallas import tpu as pltpu
from jax.sharding import PartitionSpec as P

MESH = pl.DeviceIdType.MESH
BF = jnp.bfloat16
F32 = jnp.float32
T, D, V, FB = 512, 16384, 4096, 128
TH = T // 2
TR = 32
CH = 2048
HALF = 1024
NG = 4
ROWS = 256
CODE = 32000.0
PRE_BOUND = 60.0 * 0.046875 * 2048 * 1.01
GRAD_BOUND = 6.0 * 2 / T * 1.01
NT = (((1,), (1,)), ((), ()))
NN = (((1,), (0,)), ((), ()))


def dot(a, b, dims):
    return lax.dot_general(a, b, dims, preferred_element_type=F32)


def head_kernel(
    hid_ref, w_ref, gain_ref, e_ref, tgt_ref,
    grad_ref, loss_ref,
    e_flat, w_flat, stage, hid_all, hid_t, ps, acc, core_in, ps2, mp_in, oh, ct, tcol,
    pre_s, act_s, nb, nf, dpf, sq_own, sq_in, sq_sum, sq_in2, inv_s,
    lz, lx, rx, rz, sx2, rx2, sz2, rz2, lg, tsq, st_own, st_in, sc_all, dl,
    stage_sem, out_sem,
    hid_ss, hid_rs, core_ss, core_rs, mp_ss, mp_rs, core2_ss, core2_rs, mp2_ss, mp2_rs,
    nf_ss, nf_rs, nfc_ss, nfc_rs, dp_ss, dp_rs, dpc_ss, dpc_rs,
    sq_ss, sq_rs, sq2_ss, sq2_rs, st_ss, st_rs, sc_ss, sc_rs,
    rx_ss, rx_rs, rz_ss, rz_rs, rx2_ss, rx2_rs, rz2_ss, rz2_rs,
    az_ss, az_rs, azz_ss, azz_rs, ax_ss, ax_rs, axf_ss, axf_rs, azf_ss, azf_rs, axz_ss, axz_rs,
):
    dp = lax.axis_index("dp")
    mp = lax.axis_index("mp")
    x, zl = lax.rem(dp, 4), dp // 4
    yz, c = mp // 2, lax.rem(mp, 2)
    y, zh = yz // 2, lax.rem(yz, 2)
    pos = x * 2 + zl

    def at_dp(dx, dz):
        return (lax.rem(zl + dz, 2) * 4 + lax.rem(x + dx, 4), mp)

    def at_mp(k, dc=0):
        return (dp, yz_of(k) * 2 + lax.rem(c + dc, 2))

    def yz_of(k):
        return lax.rem(y + k // 2, 4) * 2 + lax.rem(zh + k % 2, 2)

    def yz_from(k):
        return lax.rem(y + 4 - k // 2, 4) * 2 + lax.rem(zh + k % 2, 2)

    zpeer = at_dp(0, 1)
    sibling = at_mp(0, 1)
    dp_offs = [(k % 4, k // 4) for k in (6, 2, 5, 7, 1, 3, 4)]
    mp_offs = [5, 4, 3, 7, 2, 6, 1]
    mp15 = [(k, 1) for k in [*mp_offs, 0]] + [(k, 0) for k in mp_offs]

    def rc(src, dst, ss, rs, dev):
        return pltpu.make_async_remote_copy(
            src_ref=src, dst_ref=dst, send_sem=ss, recv_sem=rs, device_id=dev, device_id_type=MESH
        )

    def load_w(i):
        return pltpu.make_async_copy(w_ref.at[pl.ds(i * ROWS, ROWS)], stage.at[i], stage_sem.at[i])

    def load_e(i):
        slot = lax.rem(i, 4)
        return pltpu.make_async_copy(
            e_ref.at[pl.ds(i * ROWS, ROWS)], stage.at[slot], stage_sem.at[slot]
        )

    for i in range(4):
        load_w(i).start()

    barrier = pltpu.get_barrier_semaphore()
    for o in dp_offs:
        pl.semaphore_signal(barrier, inc=1, device_id=at_dp(*o), device_id_type=MESH)
    for k, dc in mp15:
        pl.semaphore_signal(barrier, inc=1, device_id=at_mp(k, dc), device_id_type=MESH)
    pl.semaphore_wait(barrier, len(dp_offs) + len(mp15))

    def tok(p):
        return pl.ds(pl.multiple_of(p * TR, TR), TR)

    def send_hid(q, h):
        return rc(
            hid_ref.at[pl.ds(h * TR, TR)], hid_all.at[h, tok(pos)],
            hid_ss.at[q, h], hid_rs.at[q, h], at_dp(*dp_offs[q]),
        )

    for h in (0, 1):
        for q in range(7):
            send_hid(q, h).start()
        hid_all[h, tok(pos), :] = hid_ref[h * TR : (h + 1) * TR, :]

    def relay(slot, out, first):
        def body(i, carry):
            r = pltpu.einshape("vjl->jvl", stage[slot, pl.ds(pl.multiple_of(i * 64, 64), 64)])
            s = pl.multiple_of(first + i * 64, 64)
            for j in range(16):
                at = ((j % 2) * 8 + j // 2) * FB
                out[pl.ds(s, 64), at : at + FB] = r[j]
            return carry

        lax.fori_loop(0, ROWS // 64, body, 0)

    def relay_e(i, carry):
        load_e(i).wait()
        relay(lax.rem(i, 4), e_flat, i * ROWS)

        @pl.when(i + 4 < V // ROWS)
        def _():
            load_e(i + 4).start()

        return carry

    for i in range(4):
        load_w(i).wait()
        relay(i, w_flat, i * ROWS)
        load_e(i).start()

    local_tgt = tgt_ref[...].astype(F32) - (mp * V).astype(F32)
    for i in range(4):
        part = jnp.broadcast_to(local_tgt[:, i * FB : (i + 1) * FB], (FB, FB)).T
        for j in (0, 1):
            block = i * 2 + j
            at = ((block % 4) * 2 + block // 4) * TR
            for h in (0, 1):
                first = j * 64 + h * TR
                tcol[h, at : at + TR, :] = part[first : first + TR, :]

    def zcol(i):
        return pl.ds(pl.multiple_of(i * CH, CH), HALF)

    def xcol(i):
        return pl.ds(pl.multiple_of(i * CH + HALF, HALF), HALF)

    for h in (0, 1):
        for i in (0, 1):
            ids = (lax.broadcasted_iota(jnp.int32, (TH, HALF), 1) + i * CH).astype(F32)
            want = tcol[h, :, :1]
            lz[h * 2 + i] = (ids == want).astype(BF)
            lx[h * 2 + i] = (ids + HALF == want).astype(BF)

    def pick_body(n, carry):
        col = pl.ds(pl.multiple_of(n * 256, 256), 256)
        for h in (0, 1):
            r = jnp.zeros((TH, 256), F32)
            for i in (0, 1):
                r = r + dot(lz[h * 2 + i], e_flat[i * CH : i * CH + HALF, col], NN)
                r = r + dot(lx[h * 2 + i], e_flat[i * CH + HALF : (i + 1) * CH, col], NN)
            oh[h, :, col] = r.astype(BF)
        return carry

    lax.fori_loop(0, 8, relay_e, 0)

    def core_copy(h, ss, rs, t):
        two = pl.ds(t * 2, 2)
        return rc(ps.at[h, two], core_in.at[h, two], ss.at[h, t], rs.at[h, t], sibling)

    def mp_copy(h, ss, rs, k):
        return rc(ps2.at[h, yz_of(k)], mp_in.at[h, k], ss.at[h, k], rs.at[h, k], at_mp(k))

    def product(h, tile, css, crs, side):
        who = lax.rem(c + side, 2)

        def body(t, carry):
            first = who * 8 + t * 2
            r = tile(first, pl.ds(pl.multiple_of(first * FB, 2 * FB), 2 * FB))
            if side:
                ps[h, t * 2] = r[:, :FB].astype(BF)
                ps[h, t * 2 + 1] = r[:, FB:].astype(BF)
                core_copy(h, css, crs, t).start()
            else:
                acc[h, first] = r[:, :FB]
                acc[h, first + 1] = r[:, FB:]
            return carry

        lax.fori_loop(0, 4, body, 0)

    def encode(v, bound):
        root = lax.rsqrt(lax.rsqrt(jnp.abs(v) * (CODE**4 / bound)))
        code = (root + 0.5).astype(jnp.int32)
        return jnp.where(v < 0, -code, code).astype(jnp.int16)

    def decode(code, bound):
        root = code.astype(F32) * (1.0 / CODE)
        return root * jnp.abs(root) * (root * root) * bound

    def exchange(h, css, crs, mss, mrs, bound):
        for t in range(4):
            core_copy(h, css, crs, t).wait_recv()
        for k in mp_offs:
            b = yz_of(k)
            ps2[h, b] = encode(acc[h, c * 8 + b] + core_in[h, b].astype(F32), bound)
            mp_copy(h, mss, mrs, k).start()

    def collect(h, css, crs, mss, mrs, bound):
        total = acc[h, c * 8 + yz] + core_in[h, yz].astype(F32)
        for k in mp_offs:
            mp_copy(h, mss, mrs, k).wait_recv()
            total = total + decode(mp_in[h, k], bound)
        for k in mp_offs:
            mp_copy(h, mss, mrs, k).wait_send()
        for t in range(4):
            core_copy(h, css, crs, t).wait_send()
        return total

    for h in (0, 1):
        for q in range(7):
            send_hid(q, h).wait_recv()
        for side in (1, 0):
            product(h, lambda first, col, h=h: dot(hid_all[h], w_flat[:, col], NN), core_ss, core_rs, side)
        exchange(h, core_ss, core_rs, mp_ss, mp_rs, PRE_BOUND)

    lax.fori_loop(8, V // ROWS, relay_e, 0)
    lax.fori_loop(0, 2, pick_body, 0)

    gain = gain_ref[...]

    def cols(core, b):
        return pl.ds(pl.multiple_of((core * 8 + b) * FB, FB), FB)

    def ag_copy(buf, h, ss, rs, k):
        return rc(nb.at[h], buf.at[h, :, cols(c, yz)], ss.at[h, k], rs.at[h, k], at_mp(k))

    def ag_pass(buf, h, ss, rs, k):
        at = buf.at[h, :, cols(c, yz_from(k))]
        return rc(nb.at[h] if k == 0 else at, at, ss.at[h, k], rs.at[h, k], sibling)

    def gather_start(buf, h, ss, rs, css, crs):
        for k in mp_offs:
            ag_copy(buf, h, ss, rs, k).start()
        ag_pass(buf, h, css, crs, 0).start()
        buf[h, :, cols(c, yz)] = nb[h]

    def gather_mid(buf, h, ss, rs, css, crs):
        for k in reversed(mp_offs):
            ag_copy(buf, h, ss, rs, k).wait_recv()
            ag_pass(buf, h, css, crs, k).start()

    def gather_end(buf, h, ss, rs, css, crs):
        for k in range(8):
            ag_pass(buf, h, css, crs, k).wait_recv()
        for k in range(8):
            ag_pass(buf, h, css, crs, k).wait_send()
        for k in mp_offs:
            ag_copy(buf, h, ss, rs, k).wait_send()

    nf_sems = (nf_ss, nf_rs, nfc_ss, nfc_rs)
    dp_sems = (dp_ss, dp_rs, dpc_ss, dpc_rs)

    def activate(h):
        pre = collect(h, core_ss, core_rs, mp_ss, mp_rs, PRE_BOUND)
        pre_s[h] = pre
        own = hid_all[h, :, pl.ds(pl.multiple_of(dp * FB, FB), FB)].astype(F32)
        act = own + pre / (1.0 + jnp.exp(-pre))
        act_s[h] = act
        nb[h] = (act * gain).astype(BF)
        gather_start(nf, h, *nf_sems)
        squares = act * act
        for i in (0, 1):
            row = jnp.sum(squares[i * FB : (i + 1) * FB, :].T, axis=0, keepdims=True)
            at = h * TH + i * FB
            sq_own[:, at : at + FB] = jnp.broadcast_to(row, (8, FB))

    def send_sq(q):
        k, dc = mp15[q]
        return rc(sq_own, sq_in.at[mp], sq_ss.at[q], sq_rs.at[q], at_mp(k, dc))

    activate(0)
    lax.fori_loop(2, 4, pick_body, 0)
    activate(1)
    for q in range(15):
        send_sq(q).start()
    sq_in[mp] = sq_own[...]
    lax.fori_loop(4, 6, pick_body, 0)
    gather_mid(nf, 0, *nf_sems)
    lax.fori_loop(6, 8, pick_body, 0)
    gather_end(nf, 0, *nf_sems)

    def rows_of(xx, zz):
        return tok(xx * 2 + zz)

    def xd(d):
        return lax.rem(x + d, 4)

    def rz_copy(g, d):
        return rc(
            lz.at[g, rows_of(xd(d), 1 - zl)], rz.at[g, d], rz_ss.at[g, d], rz_rs.at[g, d], zpeer
        )

    def rx_copy(g, d):
        src = lx.at[g, pl.ds(pl.multiple_of(xd(d) * 2 * TR, 2 * TR), 2 * TR)]
        return rc(src, rx.at[g, d - 1], rx_ss.at[g, d - 1], rx_rs.at[g, d - 1], at_dp(d, 0))

    def rx2_copy(g):
        return rc(sx2.at[g], rx2.at[g], rx2_ss.at[g], rx2_rs.at[g], zpeer)

    def rz2_copy(g, d):
        return rc(
            sz2.at[g, d - 1], rz2.at[g, d - 1], rz2_ss.at[g, d - 1], rz2_rs.at[g, d - 1], at_dp(d, 0)
        )

    def logits_chunk(g):
        h, i = g // 2, g % 2
        lz[g] = dot(nf[h], e_flat[i * CH : i * CH + HALF, :], NT).astype(BF)
        for d in (2, 1, 3, 0):
            rz_copy(g, d).start()
        lx[g] = dot(nf[h], e_flat[i * CH + HALF : (i + 1) * CH, :], NT).astype(BF)
        for d in (2, 1, 3):
            rx_copy(g, d).start()

    def second_step(g):
        h, i = g // 2, g % 2
        for d in (1, 3, 2):
            rx_copy(g, d).wait_recv()
        base = pl.multiple_of(x * 2 * TR, 2 * TR)
        for mine in (False, True):
            off = pl.multiple_of((zl if mine else 1 - zl) * TR, TR)
            s = lx[g, pl.ds(base + off, TR)].astype(F32)
            for d in range(3):
                s = s + rx[g, d, pl.ds(off, TR)].astype(F32)
            if mine:
                lg[h, :, xcol(i)] = s
            else:
                sx2[g] = s.astype(BF)
                rx2_copy(g).start()
        for d in (2, 1, 3, 0):
            rz_copy(g, d).wait_recv()
            s = lz[g, rows_of(xd(d), zl)].astype(F32) + rz[g, d].astype(F32)
            if d:
                sz2[g, d - 1] = s.astype(BF)
                rz2_copy(g, d).start()
            else:
                lg[h, :, zcol(i)] = s

    def rs_end(g):
        h, i = g // 2, g % 2
        rx2_copy(g).wait_recv()
        lg[h, :, xcol(i)] = lg[h, :, xcol(i)] + rx2[g].astype(F32)
        s = lg[h, :, zcol(i)]
        for d in (1, 3, 2):
            rz2_copy(g, d).wait_recv()
            s = s + rz2[g, d - 1].astype(F32)
        lg[h, :, zcol(i)] = s

    def dl_at(h, xx, zz, col):
        return dl.at[h, rows_of(xx, zz), col]

    def az_copy(g, d):
        a = dl_at(g // 2, x, zl, zcol(g % 2))
        return rc(a, a, az_ss.at[g, d - 1], az_rs.at[g, d - 1], at_dp(d, 0))

    def azz_copy(g):
        a = dl_at(g // 2, x, zl, zcol(g % 2))
        return rc(a, a, azz_ss.at[g], azz_rs.at[g], zpeer)

    def azf_copy(g, d):
        a = dl_at(g // 2, lax.rem(x + 4 - d, 4), zl, zcol(g % 2))
        return rc(a, a, azf_ss.at[g, d - 1], azf_rs.at[g, d - 1], zpeer)

    def ax_copy(g, d):
        a = dl_at(g // 2, x, zl, xcol(g % 2))
        return rc(a, a, ax_ss.at[g, d - 1], ax_rs.at[g, d - 1], at_dp(d, 0))

    def axz_copy(g):
        a = dl_at(g // 2, x, zl, xcol(g % 2))
        return rc(a, a, axz_ss.at[g], axz_rs.at[g], zpeer)

    def axf_copy(g, d):
        a = dl_at(g // 2, x, 1 - zl, xcol(g % 2))
        return rc(a, a, axf_ss.at[g, d - 1], axf_rs.at[g, d - 1], at_dp(d, 0))

    lane = lax.broadcasted_iota(jnp.int32, (TR, FB), 1)

    def send_st(h, q):
        k, dc = mp15[q]
        return rc(st_own.at[h], st_in.at[h, mp], st_ss.at[h, q], st_rs.at[h, q], at_mp(k, dc))

    def softmax(h):
        inv_own = inv_s[h, tok(pos), :][:, :1]
        want = tcol[h, tok(pos), :][:, :1]
        m = jnp.full((TR, 1), -jnp.inf, F32)
        for j in range(V // HALF):
            v = lg[h, :, j * HALF : (j + 1) * HALF] * inv_own
            lg[h, :, j * HALF : (j + 1) * HALF] = v
            m = jnp.maximum(m, jnp.max(v, axis=1, keepdims=True))
        s, sl, pk = (jnp.zeros((TR, 1), F32) for _ in range(3))
        for j in range(V // HALF):
            ids = (lax.broadcasted_iota(jnp.int32, (TR, HALF), 1) + j * HALF).astype(F32)
            v = lg[h, :, j * HALF : (j + 1) * HALF]
            p = jnp.exp(v - m)
            dl[h, tok(pos), j * HALF : (j + 1) * HALF] = p.astype(BF)
            g = h * 2 + j // 2
            if j % 2:
                axz_copy(g).start()
                for d in (2, 1, 3):
                    ax_copy(g, d).start()
            else:
                for d in (2, 1, 3):
                    az_copy(g, d).start()
                azz_copy(g).start()
            s = s + jnp.sum(p, axis=1, keepdims=True)
            sl = sl + jnp.sum(p * v, axis=1, keepdims=True)
            pk = pk + jnp.sum(jnp.where(ids == want, v, 0.0), axis=1, keepdims=True)
        tsq[...] = jnp.zeros((FB, FB), F32)
        tsq[:TR, :] = jnp.where(
            lane == 0, m, jnp.where(lane == 1, s, jnp.where(lane == 2, sl, jnp.where(lane == 3, pk, 0.0)))
        )
        st_own[h] = tsq[...].T[:8, :]
        for q in range(15):
            send_st(h, q).start()
        st_in[h, mp] = st_own[h]

    def forward(g):
        axz_copy(g).wait_recv()
        for d in (2, 1, 3):
            axf_copy(g, d).start()
        for d in (1, 3, 2):
            az_copy(g, d).wait_recv()
            azf_copy(g, d).start()

    def ag_end(g):
        azz_copy(g).wait_recv()
        for d in (1, 3, 2):
            ax_copy(g, d).wait_recv()
            axf_copy(g, d).wait_recv()
            azf_copy(g, d).wait_recv()

    def send_sc(h, q):
        a = sc_all.at[h, pos]
        return rc(a, a, sc_ss.at[h, q], sc_rs.at[h, q], at_dp(*dp_offs[q]))

    def statistics(h):
        for q in range(15):
            send_st(h, q).wait_recv()
        all_m = st_in[h, :, 0, :]
        top = jnp.max(all_m, axis=0, keepdims=True)
        scale = jnp.exp(all_m - top)
        total = jnp.sum(st_in[h, :, 1, :] * scale, axis=0, keepdims=True)
        total_l = jnp.sum(st_in[h, :, 2, :] * scale, axis=0, keepdims=True)
        picked = jnp.sum(st_in[h, :, 3, :], axis=0, keepdims=True)
        valid = lax.broadcasted_iota(jnp.int32, (1, FB), 1) < TR
        total = jnp.where(valid, total, 1.0)
        lse = top + jnp.log(total)
        moment = (total_l / total - picked) / T
        factor = jnp.exp(st_own[h, :1, :] - lse) / T
        sub = lax.broadcasted_iota(jnp.int32, (FB, FB), 0)
        table = jnp.where(sub == 0, factor, jnp.where(sub == 1, moment, jnp.where(sub == 2, lse - picked, 0.0)))
        tsq[...] = table.T
        sc_all[h, pos] = tsq[:TR, :]
        for q in range(7):
            send_sc(h, q).start()

    def factors(h):
        for q in range(7):
            send_sc(h, q).wait_recv()
        for b in range(8):
            ct[h, b * TR : (b + 1) * TR, :] = jnp.broadcast_to(sc_all[h, b][:, 0:1], (TR, FB))

    def scaled_tile(h, first, col, r):
        f = ct[h]
        own_row = oh[h, :, col].astype(F32) / T
        return jnp.concatenate(
            [r[:, b * FB : (b + 1) * FB] * f - own_row[:, b * FB : (b + 1) * FB] for b in (0, 1)], axis=1
        )

    def early_part(h):
        def body(t, carry):
            r = dot(dl[h, :, :CH], e_flat[:CH, pl.ds(pl.multiple_of(t * 256, 256), 256)], NN)
            acc[h, t * 2] = r[:, :FB]
            acc[h, t * 2 + 1] = r[:, FB:]
            return carry

        lax.fori_loop(0, 8, body, 0)

    def late_tile(h):
        def tile(first, col):
            r = dot(dl[h, :, CH:], e_flat[CH:, col], NN)
            return scaled_tile(h, first, col, r + jnp.concatenate([acc[h, first], acc[h, first + 1]], axis=1))

        return tile

    def whole_tile(h):
        return lambda first, col: scaled_tile(h, first, col, dot(dl[h], e_flat[:, col], NN))

    def pre_gradient(h):
        dnormed = collect(h, core2_ss, core2_rs, mp2_ss, mp2_rs, GRAD_BOUND)
        moments = jnp.concatenate([sc_all[h, b][:, 1:2] for b in range(8)], axis=0)
        inv, act, pre = inv_s[h], act_s[h], pre_s[h]
        dact = inv * gain * dnormed - act * (inv * inv * (moments / D))
        sig = 1.0 / (1.0 + jnp.exp(-pre))
        nb[h] = (dact * sig * (1.0 + pre * (1.0 - sig))).astype(BF)
        gather_start(dpf, h, *dp_sems)

    logits_chunk(0)
    logits_chunk(1)
    gather_mid(nf, 1, *nf_sems)
    second_step(0)
    gather_end(nf, 1, *nf_sems)
    logits_chunk(2)
    second_step(1)
    logits_chunk(3)

    def send_sq2(q):
        return rc(sq_sum, sq_in2.at[dp], sq2_ss.at[q], sq2_rs.at[q], at_dp(*dp_offs[q]))

    for q in range(15):
        send_sq(q).wait_recv()
    sq_sum[...] = jnp.sum(sq_in[...], axis=0)
    for q in range(7):
        send_sq2(q).start()
    sq_in2[dp] = sq_sum[...]
    for h in (0, 1):
        for i in range(8):
            hid_t[i * FB : (i + 1) * FB, h * TH : (h + 1) * TH] = hid_all[h, :, i * FB : (i + 1) * FB].T

    second_step(2)
    for q in range(7):
        send_sq2(q).wait_recv()
    mean = jnp.sum(sq_in2[...], axis=0)[:1, :] / D
    inv_row = lax.rsqrt(mean + 1e-05)
    for h in (0, 1):
        for i in (0, 1):
            at = h * TH + i * FB
            inv_s[h, i * FB : (i + 1) * FB, :] = jnp.broadcast_to(inv_row[:, at : at + FB], (FB, FB)).T

    rs_end(0)
    rs_end(1)
    softmax(0)
    second_step(3)
    forward(0)
    rs_end(2)
    rs_end(3)
    softmax(1)
    forward(1)
    statistics(0)
    ag_end(0)
    ag_end(1)
    factors(0)
    product(0, whole_tile(0), core2_ss, core2_rs, 1)
    forward(2)
    product(0, whole_tile(0), core2_ss, core2_rs, 0)
    exchange(0, core2_ss, core2_rs, mp2_ss, mp2_rs, GRAD_BOUND)
    statistics(1)
    forward(3)
    ag_end(2)
    early_part(1)
    pre_gradient(0)
    factors(1)
    ag_end(3)
    product(1, late_tile(1), core2_ss, core2_rs, 1)
    gather_mid(dpf, 0, *dp_sems)
    product(1, late_tile(1), core2_ss, core2_rs, 0)
    exchange(1, core2_ss, core2_rs, mp2_ss, mp2_rs, GRAD_BOUND)
    loss = jnp.zeros((TR, 1), F32)
    for h in (0, 1):
        for b in range(8):
            loss = loss + sc_all[h, b][:, 2:3]
    loss_ref[...] = jnp.sum(loss, axis=0, keepdims=True) / T
    gather_end(dpf, 0, *dp_sems)
    pre_gradient(1)

    def grad_copy(n, col):
        return pltpu.make_async_copy(w_flat.at[:, col], grad_ref.at[:, col], out_sem.at[n])

    def grad_tile(n, core, dy):
        first = core * 8 + lax.rem(y + 4 - dy, 4) * 2
        col = pl.ds(pl.multiple_of(first * FB, 2 * FB), 2 * FB)
        r = dot(hid_t[:, :TH], dpf[0, :, col], NN) + dot(hid_t[:, TH:], dpf[1, :, col], NN)
        w_flat[:, col] = r.astype(BF)
        grad_copy(n, col).start()
        return n, col

    tiles = []
    for dy in (0, 1, 3, 2):
        for k in (dy * 2, dy * 2 + 1):
            if k:
                ag_copy(dpf, 1, dp_ss, dp_rs, k).wait_recv()
                ag_pass(dpf, 1, dpc_ss, dpc_rs, k).start()
        tiles.append(grad_tile(len(tiles), c, dy))
    for dy in (0, 1, 3, 2):
        for k in (dy * 2, dy * 2 + 1):
            ag_pass(dpf, 1, dpc_ss, dpc_rs, k).wait_recv()
        tiles.append(grad_tile(len(tiles), 1 - c, dy))
    for k in range(8):
        ag_pass(dpf, 1, dpc_ss, dpc_rs, k).wait_send()
    for k in mp_offs:
        ag_copy(dpf, 1, dp_ss, dp_rs, k).wait_send()

    for q in range(7):
        send_sq2(q).wait_send()
        for h in (0, 1):
            send_hid(q, h).wait_send()
            send_sc(h, q).wait_send()
    for q in range(15):
        send_sq(q).wait_send()
        for h in (0, 1):
            send_st(h, q).wait_send()

    def drain(g, carry):
        rx2_copy(g).wait_send()
        azz_copy(g).wait_send()
        axz_copy(g).wait_send()
        for d in range(4):
            rz_copy(g, d).wait_send()
        for d in (1, 2, 3):
            rx_copy(g, d).wait_send()
            rz2_copy(g, d).wait_send()
            az_copy(g, d).wait_send()
            azf_copy(g, d).wait_send()
            ax_copy(g, d).wait_send()
            axf_copy(g, d).wait_send()
        return carry

    lax.fori_loop(0, NG, drain, 0)
    for n, col in tiles:
        grad_copy(n, col).wait()


def head(hidden, weight, gain, embed, targets):
    vm = pltpu.VMEM
    dma = pltpu.SemaphoreType.DMA
    scratch = [
        vm((V, 2048), BF), vm((1024, 2048), BF), vm((4, ROWS, 16, FB), BF), vm((2, TH, 1024), BF), vm((1024, T), BF),
        vm((2, 8, TH, FB), BF), vm((2, 16, TH, FB), F32), vm((2, 8, TH, FB), BF), vm((2, 8, TH, FB), jnp.int16),
        vm((2, 8, TH, FB), jnp.int16), vm((2, TH, 2048), BF), vm((2, TH, FB), F32), vm((2, TH, FB), F32),
        vm((2, TH, FB), F32), vm((2, TH, FB), F32), vm((2, TH, FB), BF), vm((2, TH, 2048), BF), vm((2, TH, 2048), BF),
        vm((8, T), F32), vm((16, 8, T), F32), vm((8, T), F32), vm((8, 8, T), F32), vm((2, TH, FB), F32),
        vm((NG, TH, HALF), BF), vm((NG, TH, HALF), BF),
        vm((NG, 3, 2 * TR, HALF), BF), vm((NG, 4, TR, HALF), BF),
        vm((NG, TR, HALF), BF), vm((NG, TR, HALF), BF), vm((NG, 3, TR, HALF), BF), vm((NG, 3, TR, HALF), BF),
        vm((2, TR, V), F32), vm((FB, FB), F32), vm((2, 8, FB), F32), vm((2, 16, 8, FB), F32),
        vm((2, 8, TR, FB), F32), vm((2, TH, V), BF),
        dma((4,)), dma((8,)),
    ]
    counts = [
        (7, 2), (2, 4), (2, 8), (2, 4), (2, 8), (2, 8), (2, 8), (2, 8), (2, 8), (15,), (7,), (2, 15), (2, 7),
        (NG, 3), (NG, 4), (NG,), (NG, 3),
        (NG, 3), (NG,), (NG, 3), (NG, 3), (NG, 3), (NG,),
    ]
    for n in counts:
        scratch += [dma(n), dma(n)]
    vspec = pl.BlockSpec(memory_space=pltpu.VMEM)
    anyspec = pl.BlockSpec(memory_space=pl.ANY)
    return pl.pallas_call(
        head_kernel,
        name="head",
        out_shape=(jax.ShapeDtypeStruct((1024, 2048), BF), jax.ShapeDtypeStruct((1, 1), F32)),
        in_specs=[vspec, anyspec, vspec, anyspec, vspec],
        out_specs=(anyspec, vspec),
        scratch_shapes=scratch,
        compiler_params=pltpu.CompilerParams(
            collective_id=0, has_side_effects=True, vmem_limit_bytes=62 << 20
        ),
    )(hidden, weight, gain, embed, targets)


def order_kernel(grad, out):
    blocks = jnp.stack([grad[:, ((j % 2) * 8 + j // 2) * FB :][:, :FB] for j in range(16)])
    out[...] = pltpu.einshape("jvl->vjl", blocks)


def in_order(grad):
    rows = 128
    return pl.pallas_call(
        order_kernel,
        name="in_order",
        grid=(1024 // rows,),
        out_shape=jax.ShapeDtypeStruct((1024, 16, FB), BF),
        in_specs=[pl.BlockSpec((rows, 2048), lambda i: (i, 0))],
        out_specs=pl.BlockSpec((rows, 16, FB), lambda i: (i, 0, 0)),
        compiler_params=pltpu.CompilerParams(vmem_limit_bytes=62 << 20),
    )(grad)


def on_device(hidden_rows, head_weight, norm_gain, vocab_embed, targets):
    grad, loss = head(
        hidden_rows,
        head_weight.reshape(1024, 16, FB),
        norm_gain.reshape(1, FB),
        vocab_embed.reshape(V, 16, FB),
        targets.reshape(1, T),
    )
    return in_order(grad).reshape(head_weight.shape), loss.reshape(())


def solution(mesh):
    return jax.shard_map(
        on_device,
        mesh=mesh,
        in_specs=(
            P("dp", "mp"),
            P("mp", None, "dp", None),
            P("mp", "dp", None),
            P("mp", None, "dp", None),
            P(),
        ),
        out_specs=(P("mp", None, "dp", None), P()),
        check_vma=False,
    )
```

time: 709 us -> 178 us (0.25)
  waiting for transfers between devices: 412 us -> 0 us
  blocking collectives: 217 us -> 0 us
  Pallas kernels: 0 us -> 175 us
  matrix products: 43.1 us -> 0 us
  between operations: 15.9 us -> 2.38 us
  other arithmetic: 12.4 us -> 0 us
  local copies, waits for them, and re-layouts: 8.1 us -> 0 us
    reduce_scatter x3 -> x0, waiting for transfers between devices: 250 us -> none  [the longest x1 90.3 us: on_device(): lax.psum_scatter(lax.dot_general(columns, embed_flat, contract, preferred...]
    psum x4 -> x0, blocking collectives: 183 us -> none  [the longest x1 65.7 us: on_device(): squares = lax.psum(jnp.sum(act * act, axis=0), ('dp', 'mp'))]
    pallas_call x0 -> x2, Pallas kernels: none -> 175 us  [the longest x1 168 us: head(): pl.pallas_call(head_kernel, name='head', out_shape=(jax.ShapeDtypeStruct(...]
    all_gather x4 -> x0, waiting for transfers between devices: 161 us -> none  [the longest x1 46.6 us: on_device(): all_dlogits = lax.all_gather(dlogits, 'dp', axis=0, tiled=True)]
    dot_general x4 -> x0, matrix products: 43.1 us -> none  [the longest x1 15.2 us: on_device(): lax.dot_general(columns, embed_flat, contract, preferred_element_type=jnp...]
    pmax x1 -> x0, blocking collectives: 33.2 us -> none  [on_device(): top = lax.pmax(local_max, 'mp')]
    unnamed x8 -> x0, local copies, waits for them, and re-layouts: 8.07 us -> none
  transfers between devices with their start and end apart: 7 -> 0, of which waited for: 7 -> 0; matrix products, arithmetic and copies ran while one was open for 0% -> 0% of each run, Pallas kernels for 0% -> 0%
where the time goes in v3:
time: 178 us
  Pallas kernels  175 us (98%)
  between operations  2.38 us (1%)
    pallas_call x1, Pallas kernels, head(): pl.pallas_call(head_kernel, name='head', out_shape=(jax.ShapeDtypeStruct(...  168 us
    pallas_call x1, Pallas kernels, in_order(): pl.pallas_call(order_kernel, name='in_order', grid=(1024 // rows,), out_s...  6.93 us

profile of v3, /device:TPU:1, one launch (start us, length us, event | category | flops | bytes accessed | tf_op | source)
XLA Modules:
  0.0 177.7 jit_solution(12582178106400373343)
XLA Ops:
  0.6 168.4 %head.1 = (bf16[1024,2048]{1,0:T(8,128)(2,1)}, f32[1,1]{1,0:T(1,128)}) custom-call(bf16[64,1024]{1,0:T(8,128)(2,1)} %hid_ref.1, bf16[1024,16,128]{2,1,0:T(8,128)(2,1)} %bitcast.9, f32[1,128]{1,0:T(1,128)} %bitcast.12, bf16[4096,16,128]{2,1,0:T(8,128)(2,1)} %bitcast.8, s32[1,512]{1,0:T(1,128)} %bitcast.11), custom_call_target="tpu_custom_call" | custom-call | tf_op jit(solution)/shard_map/head/pallas_call | solution.py:656
  169.0 6.9 %in_order.1 = bf16[1024,16,128]{2,1,0:T(8,128)(2,1)} custom-call(bf16[1024,2048]{1,0:T(8,128)(2,1)} %get-tuple-element.4.grad), custom_call_target="tpu_custom_call" | custom-call | tf_op jit(solution)/shard_map/in_order/pallas_call | solution.py:676

commit v4 on v3

--- a/solution.py
+++ b/solution.py
@@ -503,66 +503,69 @@
         nb[h] = (dact * sig * (1.0 + pre * (1.0 - sig))).astype(BF)
         gather_start(dpf, h, *dp_sems)
 
+    def send_sq2(q):
+        return rc(sq_sum, sq_in2.at[dp], sq2_ss.at[q], sq2_rs.at[q], at_dp(*dp_offs[q]))
+
+    def send_squares():
+        for q in range(15):
+            send_sq(q).wait_recv()
+        sq_sum[...] = jnp.sum(sq_in[...], axis=0)
+        for q in range(7):
+            send_sq2(q).start()
+        sq_in2[dp] = sq_sum[...]
+
+    def norms():
+        for q in range(7):
+            send_sq2(q).wait_recv()
+        mean = jnp.sum(sq_in2[...], axis=0)[:1, :] / D
+        inv_row = lax.rsqrt(mean + 1e-05)
+        for h in (0, 1):
+            for i in (0, 1):
+                at = h * TH + i * FB
+                inv_s[h, i * FB : (i + 1) * FB, :] = jnp.broadcast_to(inv_row[:, at : at + FB], (FB, FB)).T
+
     logits_chunk(0)
     logits_chunk(1)
     gather_mid(nf, 1, *nf_sems)
-    second_step(0)
+    send_squares()
     gather_end(nf, 1, *nf_sems)
     logits_chunk(2)
+    second_step(0)
+    logits_chunk(3)
     second_step(1)
-    logits_chunk(3)
-
-    def send_sq2(q):
-        return rc(sq_sum, sq_in2.at[dp], sq2_ss.at[q], sq2_rs.at[q], at_dp(*dp_offs[q]))
-
-    for q in range(15):
-        send_sq(q).wait_recv()
-    sq_sum[...] = jnp.sum(sq_in[...], axis=0)
-    for q in range(7):
-        send_sq2(q).start()
-    sq_in2[dp] = sq_sum[...]
-    for h in (0, 1):
-        for i in range(8):
-            hid_t[i * FB : (i + 1) * FB, h * TH : (h + 1) * TH] = hid_all[h, :, i * FB : (i + 1) * FB].T
-
+    norms()
     second_step(2)
-    for q in range(7):
-        send_sq2(q).wait_recv()
-    mean = jnp.sum(sq_in2[...], axis=0)[:1, :] / D
-    inv_row = lax.rsqrt(mean + 1e-05)
-    for h in (0, 1):
-        for i in (0, 1):
-            at = h * TH + i * FB
-            inv_s[h, i * FB : (i + 1) * FB, :] = jnp.broadcast_to(inv_row[:, at : at + FB], (FB, FB)).T
-
     rs_end(0)
     rs_end(1)
     softmax(0)
     second_step(3)
     forward(0)
+    forward(1)
     rs_end(2)
     rs_end(3)
     softmax(1)
-    forward(1)
     statistics(0)
     ag_end(0)
     ag_end(1)
     factors(0)
     product(0, whole_tile(0), core2_ss, core2_rs, 1)
-    forward(2)
     product(0, whole_tile(0), core2_ss, core2_rs, 0)
     exchange(0, core2_ss, core2_rs, mp2_ss, mp2_rs, GRAD_BOUND)
+    forward(2)
+    forward(3)
     statistics(1)
-    forward(3)
+    pre_gradient(0)
     ag_end(2)
     early_part(1)
-    pre_gradient(0)
     factors(1)
     ag_end(3)
     product(1, late_tile(1), core2_ss, core2_rs, 1)
     gather_mid(dpf, 0, *dp_sems)
     product(1, late_tile(1), core2_ss, core2_rs, 0)
     exchange(1, core2_ss, core2_rs, mp2_ss, mp2_rs, GRAD_BOUND)
+    for h in (0, 1):
+        for i in range(8):
+            hid_t[i * FB : (i + 1) * FB, h * TH : (h + 1) * TH] = hid_all[h, :, i * FB : (i + 1) * FB].T
     loss = jnp.zeros((TR, 1), F32)
     for h in (0, 1):
         for b in range(8):
@@ -672,7 +675,7 @@
 
 
 def in_order(grad):
-    rows = 128
+    rows = 512
     return pl.pallas_call(
         order_kernel,
         name="in_order",

time: 178 us -> 180 us (1.011)
  Pallas kernels: 175 us -> 177 us
    pallas_call x1, Pallas kernels: 168 us -> 173 us  [head(): pl.pallas_call(head_kernel, name='head', out_shape=(jax.ShapeDtypeStruct(...]
    pallas_call x1, Pallas kernels: 6.93 us -> 4.21 us  [in_order(): pl.pallas_call(order_kernel, name='in_order', grid=(1024 // rows,), out_s...]
where the time goes in v4:
time: 180 us; the launch traced here: 179 us
  Pallas kernels  177 us (98%)
  between operations  2.38 us (1%)
    pallas_call x1, Pallas kernels, head(): pl.pallas_call(head_kernel, name='head', out_shape=(jax.ShapeDtypeStruct(...  173 us
    pallas_call x1, Pallas kernels, in_order(): pl.pallas_call(order_kernel, name='in_order', grid=(1024 // rows,), out_s...  4.21 us

profile of v4, /device:TPU:1, one launch (start us, length us, event | category | flops | bytes accessed | tf_op | source)
XLA Modules:
  0.0 179.4 jit_solution(13641690438698795098)
XLA Ops:
  0.6 172.8 %head.1 = (bf16[1024,2048]{1,0:T(8,128)(2,1)}, f32[1,1]{1,0:T(1,128)}) custom-call(bf16[64,1024]{1,0:T(8,128)(2,1)} %hid_ref.1, bf16[1024,16,128]{2,1,0:T(8,128)(2,1)} %bitcast.9, f32[1,128]{1,0:T(1,128)} %bitcast.12, bf16[4096,16,128]{2,1,0:T(8,128)(2,1)} %bitcast.8, s32[1,512]{1,0:T(1,128)} %bitcast.11), custom_call_target="tpu_custom_call" | custom-call | tf_op jit(solution)/shard_map/head/pallas_call | solution.py:659
  173.5 4.2 %in_order.1 = bf16[1024,16,128]{2,1,0:T(8,128)(2,1)} custom-call(bf16[1024,2048]{1,0:T(8,128)(2,1)} %get-tuple-element.4.grad), custom_call_target="tpu_custom_call" | custom-call | tf_op jit(solution)/shard_map/in_order/pallas_call | solution.py:679

commit v5 on v4

--- a/solution.py
+++ b/solution.py
@@ -31,13 +31,15 @@
     grad_ref, loss_ref,
     e_flat, w_flat, stage, hid_all, hid_t, ps, acc, core_in, ps2, mp_in, oh, ct, tcol,
     pre_s, act_s, nb, nf, dpf, sq_own, sq_in, sq_sum, sq_in2, inv_s,
-    lz, lx, rx, rz, sx2, rx2, sz2, rz2, lg, tsq, st_own, st_in, sc_all, dl,
+    lz, lx, rx, rxf, sxc, rz, sx2, rx2, szf, szn, rzf, szc, rz2, lg, tsq, st_own, st_in, sc_all, dl,
     stage_sem, out_sem,
     hid_ss, hid_rs, core_ss, core_rs, mp_ss, mp_rs, core2_ss, core2_rs, mp2_ss, mp2_rs,
     nf_ss, nf_rs, nfc_ss, nfc_rs, dp_ss, dp_rs, dpc_ss, dpc_rs,
     sq_ss, sq_rs, sq2_ss, sq2_rs, st_ss, st_rs, sc_ss, sc_rs,
-    rx_ss, rx_rs, rz_ss, rz_rs, rx2_ss, rx2_rs, rz2_ss, rz2_rs,
-    az_ss, az_rs, azz_ss, azz_rs, ax_ss, ax_rs, axf_ss, axf_rs, azf_ss, azf_rs, axz_ss, axz_rs,
+    rxf_ss, rxf_rs, rxn_ss, rxn_rs, rxc_ss, rxc_rs, rz_ss, rz_rs, rx2_ss, rx2_rs,
+    rzf_ss, rzf_rs, rzn_ss, rzn_rs, rzc_ss, rzc_rs,
+    az_ss, az_rs, azh_ss, azh_rs, azz_ss, azz_rs, azf_ss, azf_rs, ax_ss, ax_rs, axh_ss, axh_rs,
+    axz_ss, axz_rs, axf_ss, axf_rs, axg_ss, axg_rs,
 ):
     dp = lax.axis_index("dp")
     mp = lax.axis_index("mp")
@@ -299,87 +301,155 @@
             lz.at[g, rows_of(xd(d), 1 - zl)], rz.at[g, d], rz_ss.at[g, d], rz_rs.at[g, d], zpeer
         )
 
-    def rx_copy(g, d):
-        src = lx.at[g, pl.ds(pl.multiple_of(xd(d) * 2 * TR, 2 * TR), 2 * TR)]
-        return rc(src, rx.at[g, d - 1], rx_ss.at[g, d - 1], rx_rs.at[g, d - 1], at_dp(d, 0))
+    def way(k):
+        return at_dp(1 if k == 0 else 3, 0)
+
+    def to(k):
+        return xd(1 if k == 0 else 3)
+
+    def source(k):
+        return xd(3 if k == 0 else 1)
+
+    def block(xx, half):
+        return pl.ds(pl.multiple_of(xx * 2 * TR + half * TR, TR), TR)
+
+    def part(half):
+        return pl.ds(half * (TR // 2), TR // 2)
+
+    def pair(ss, rs, g, k):
+        return (ss.at[g, k], rs.at[g, k], way(k))
+
+    def rxf_copy(g, k):
+        return rc(lx.at[g, block(xd(2), k)], rxf.at[g, k], *pair(rxf_ss, rxf_rs, g, k))
+
+    def rxn_copy(g, k):
+        here = pl.ds((1 - k) * TR, TR)
+        return rc(lx.at[g, block(to(k), 1 - k)], rx.at[g, k, here], *pair(rxn_ss, rxn_rs, g, k))
+
+    def rxc_copy(g, k):
+        return rc(sxc.at[g, k], rx.at[g, k, pl.ds(k * TR, TR)], *pair(rxc_ss, rxc_rs, g, k))
 
     def rx2_copy(g):
         return rc(sx2.at[g], rx2.at[g], rx2_ss.at[g], rx2_rs.at[g], zpeer)
 
-    def rz2_copy(g, d):
-        return rc(
-            sz2.at[g, d - 1], rz2.at[g, d - 1], rz2_ss.at[g, d - 1], rz2_rs.at[g, d - 1], at_dp(d, 0)
-        )
+    def rzf_copy(g, k):
+        return rc(szf.at[g, part(k)], rzf.at[g, k], *pair(rzf_ss, rzf_rs, g, k))
+
+    def rzn_copy(g, k):
+        return rc(szn.at[g, k], rz2.at[g, k, part(1 - k)], *pair(rzn_ss, rzn_rs, g, k))
+
+    def rzc_copy(g, k):
+        return rc(szc.at[g, k], rz2.at[g, k, part(k)], *pair(rzc_ss, rzc_rs, g, k))
 
     def logits_chunk(g):
         h, i = g // 2, g % 2
+        lx[g] = dot(nf[h], e_flat[i * CH + HALF : (i + 1) * CH, :], NT).astype(BF)
+        for k in (0, 1):
+            rxf_copy(g, k).start()
+        for k in (0, 1):
+            rxn_copy(g, k).start()
         lz[g] = dot(nf[h], e_flat[i * CH : i * CH + HALF, :], NT).astype(BF)
         for d in (2, 1, 3, 0):
             rz_copy(g, d).start()
-        lx[g] = dot(nf[h], e_flat[i * CH + HALF : (i + 1) * CH, :], NT).astype(BF)
-        for d in (2, 1, 3):
-            rx_copy(g, d).start()
+
+    def combine_x(g):
+        for k in (0, 1):
+            rxf_copy(g, k).wait_recv()
+            sxc[g, k] = (lx[g, block(to(k), k)].astype(F32) + rxf[g, k].astype(F32)).astype(BF)
+            rxc_copy(g, k).start()
+
+    def z_sum(g, d, rows):
+        first = pl.multiple_of((xd(d) * 2 + zl) * TR + rows[0], TR // 2)
+        return lz[g, pl.ds(first, rows[1])].astype(F32) + rz[g, d, rows[0] : rows[0] + rows[1]].astype(F32)
 
     def second_step(g):
         h, i = g // 2, g % 2
-        for d in (1, 3, 2):
-            rx_copy(g, d).wait_recv()
-        base = pl.multiple_of(x * 2 * TR, 2 * TR)
+        rz_copy(g, 2).wait_recv()
+        szf[g] = z_sum(g, 2, (0, TR)).astype(BF)
+        for k in (0, 1):
+            rzf_copy(g, k).start()
+        for k in (0, 1):
+            d = 1 if k == 0 else 3
+            rz_copy(g, d).wait_recv()
+            szn[g, k] = z_sum(g, d, ((1 - k) * (TR // 2), TR // 2)).astype(BF)
+            rzn_copy(g, k).start()
+        rz_copy(g, 0).wait_recv()
+        lg[h, :, zcol(i)] = z_sum(g, 0, (0, TR))
+        for k in (0, 1):
+            rxn_copy(g, k).wait_recv()
+            rxc_copy(g, k).wait_recv()
         for mine in (False, True):
-            off = pl.multiple_of((zl if mine else 1 - zl) * TR, TR)
-            s = lx[g, pl.ds(base + off, TR)].astype(F32)
-            for d in range(3):
-                s = s + rx[g, d, pl.ds(off, TR)].astype(F32)
+            zz = zl if mine else 1 - zl
+            off = pl.multiple_of(zz * TR, TR)
+            s = lx[g, block(x, zz)].astype(F32)
+            for k in (0, 1):
+                s = s + rx[g, k, pl.ds(off, TR)].astype(F32)
             if mine:
                 lg[h, :, xcol(i)] = s
             else:
                 sx2[g] = s.astype(BF)
                 rx2_copy(g).start()
-        for d in (2, 1, 3, 0):
-            rz_copy(g, d).wait_recv()
-            s = lz[g, rows_of(xd(d), zl)].astype(F32) + rz[g, d].astype(F32)
-            if d:
-                sz2[g, d - 1] = s.astype(BF)
-                rz2_copy(g, d).start()
-            else:
-                lg[h, :, zcol(i)] = s
+
+    def combine_z(g):
+        for k in (0, 1):
+            rzf_copy(g, k).wait_recv()
+            own = z_sum(g, 1 if k == 0 else 3, (k * (TR // 2), TR // 2))
+            szc[g, k] = (own + rzf[g, k].astype(F32)).astype(BF)
+            rzc_copy(g, k).start()
 
     def rs_end(g):
         h, i = g // 2, g % 2
         rx2_copy(g).wait_recv()
         lg[h, :, xcol(i)] = lg[h, :, xcol(i)] + rx2[g].astype(F32)
         s = lg[h, :, zcol(i)]
-        for d in (1, 3, 2):
-            rz2_copy(g, d).wait_recv()
-            s = s + rz2[g, d - 1].astype(F32)
+        for k in (0, 1):
+            rzn_copy(g, k).wait_recv()
+            rzc_copy(g, k).wait_recv()
+            s = s + rz2[g, k].astype(F32)
         lg[h, :, zcol(i)] = s
 
     def dl_at(h, xx, zz, col):
         return dl.at[h, rows_of(xx, zz), col]
 
-    def az_copy(g, d):
+    def half_at(h, xx, zz, k, col):
+        first = pl.multiple_of((xx * 2 + zz) * TR + k * (TR // 2), TR // 2)
+        return dl.at[h, pl.ds(first, TR // 2), col]
+
+    def az_copy(g, k):
         a = dl_at(g // 2, x, zl, zcol(g % 2))
-        return rc(a, a, az_ss.at[g, d - 1], az_rs.at[g, d - 1], at_dp(d, 0))
+        return rc(a, a, *pair(az_ss, az_rs, g, k))
+
+    def azh_copy(g, k):
+        a = half_at(g // 2, source(k), zl, k, zcol(g % 2))
+        return rc(a, a, *pair(azh_ss, azh_rs, g, k))
 
     def azz_copy(g):
         a = dl_at(g // 2, x, zl, zcol(g % 2))
         return rc(a, a, azz_ss.at[g], azz_rs.at[g], zpeer)
 
     def azf_copy(g, d):
-        a = dl_at(g // 2, lax.rem(x + 4 - d, 4), zl, zcol(g % 2))
+        a = dl_at(g // 2, xd(d), zl, zcol(g % 2))
         return rc(a, a, azf_ss.at[g, d - 1], azf_rs.at[g, d - 1], zpeer)
 
-    def ax_copy(g, d):
+    def ax_copy(g, k):
         a = dl_at(g // 2, x, zl, xcol(g % 2))
-        return rc(a, a, ax_ss.at[g, d - 1], ax_rs.at[g, d - 1], at_dp(d, 0))
+        return rc(a, a, *pair(ax_ss, ax_rs, g, k))
+
+    def axh_copy(g, k):
+        a = half_at(g // 2, source(k), zl, k, xcol(g % 2))
+        return rc(a, a, *pair(axh_ss, axh_rs, g, k))
 
     def axz_copy(g):
         a = dl_at(g // 2, x, zl, xcol(g % 2))
         return rc(a, a, axz_ss.at[g], axz_rs.at[g], zpeer)
 
-    def axf_copy(g, d):
+    def axf_copy(g, k):
         a = dl_at(g // 2, x, 1 - zl, xcol(g % 2))
-        return rc(a, a, axf_ss.at[g, d - 1], axf_rs.at[g, d - 1], at_dp(d, 0))
+        return rc(a, a, *pair(axf_ss, axf_rs, g, k))
+
+    def axg_copy(g, k):
+        a = half_at(g // 2, source(k), 1 - zl, k, xcol(g % 2))
+        return rc(a, a, *pair(axg_ss, axg_rs, g, k))
 
     lane = lax.broadcasted_iota(jnp.int32, (TR, FB), 1)
 
@@ -404,11 +474,11 @@
             g = h * 2 + j // 2
             if j % 2:
                 axz_copy(g).start()
-                for d in (2, 1, 3):
-                    ax_copy(g, d).start()
+                for k in (0, 1):
+                    ax_copy(g, k).start()
             else:
-                for d in (2, 1, 3):
-                    az_copy(g, d).start()
+                for k in (0, 1):
+                    az_copy(g, k).start()
                 azz_copy(g).start()
             s = s + jnp.sum(p, axis=1, keepdims=True)
             sl = sl + jnp.sum(p * v, axis=1, keepdims=True)
@@ -424,17 +494,30 @@
 
     def forward(g):
         axz_copy(g).wait_recv()
-        for d in (2, 1, 3):
-            axf_copy(g, d).start()
-        for d in (1, 3, 2):
-            az_copy(g, d).wait_recv()
-            azf_copy(g, d).start()
+        for k in (0, 1):
+            axf_copy(g, k).start()
+        for k in (0, 1):
+            az_copy(g, k).wait_recv()
+            azh_copy(g, k).start()
+            azf_copy(g, 3 if k == 0 else 1).start()
+        for k in (0, 1):
+            ax_copy(g, k).wait_recv()
+            axh_copy(g, k).start()
+
+    def forward_far(g):
+        for k in (0, 1):
+            axf_copy(g, k).wait_recv()
+            axg_copy(g, k).start()
+        for k in (0, 1):
+            azh_copy(g, k).wait_recv()
+        azf_copy(g, 2).start()
 
     def ag_end(g):
         azz_copy(g).wait_recv()
-        for d in (1, 3, 2):
-            ax_copy(g, d).wait_recv()
-            axf_copy(g, d).wait_recv()
+        for k in (0, 1):
+            axh_copy(g, k).wait_recv()
+            axg_copy(g, k).wait_recv()
+        for d in (1, 2, 3):
             azf_copy(g, d).wait_recv()
 
     def send_sc(h, q):
@@ -527,32 +610,44 @@
     logits_chunk(0)
     logits_chunk(1)
     gather_mid(nf, 1, *nf_sems)
+    combine_x(0)
     send_squares()
     gather_end(nf, 1, *nf_sems)
     logits_chunk(2)
+    combine_x(1)
     second_step(0)
     logits_chunk(3)
+    combine_x(2)
     second_step(1)
+    combine_z(0)
     norms()
+    combine_x(3)
     second_step(2)
+    combine_z(1)
     rs_end(0)
     rs_end(1)
     softmax(0)
     second_step(3)
+    combine_z(2)
+    combine_z(3)
     forward(0)
     forward(1)
     rs_end(2)
     rs_end(3)
     softmax(1)
+    forward_far(0)
+    forward_far(1)
     statistics(0)
     ag_end(0)
     ag_end(1)
     factors(0)
     product(0, whole_tile(0), core2_ss, core2_rs, 1)
-    product(0, whole_tile(0), core2_ss, core2_rs, 0)
-    exchange(0, core2_ss, core2_rs, mp2_ss, mp2_rs, GRAD_BOUND)
     forward(2)
     forward(3)
+    product(0, whole_tile(0), core2_ss, core2_rs, 0)
+    forward_far(2)
+    exchange(0, core2_ss, core2_rs, mp2_ss, mp2_rs, GRAD_BOUND)
+    forward_far(3)
     statistics(1)
     pre_gradient(0)
     ag_end(2)
@@ -618,12 +713,20 @@
         for d in range(4):
             rz_copy(g, d).wait_send()
         for d in (1, 2, 3):
-            rx_copy(g, d).wait_send()
-            rz2_copy(g, d).wait_send()
-            az_copy(g, d).wait_send()
             azf_copy(g, d).wait_send()
-            ax_copy(g, d).wait_send()
-            axf_copy(g, d).wait_send()
+        for k in (0, 1):
+            rxf_copy(g, k).wait_send()
+            rxn_copy(g, k).wait_send()
+            rxc_copy(g, k).wait_send()
+            rzf_copy(g, k).wait_send()
+            rzn_copy(g, k).wait_send()
+            rzc_copy(g, k).wait_send()
+            az_copy(g, k).wait_send()
+            azh_copy(g, k).wait_send()
+            ax_copy(g, k).wait_send()
+            axh_copy(g, k).wait_send()
+            axf_copy(g, k).wait_send()
+            axg_copy(g, k).wait_send()
         return carry
 
     lax.fori_loop(0, NG, drain, 0)
@@ -641,16 +744,17 @@
         vm((2, TH, FB), F32), vm((2, TH, FB), F32), vm((2, TH, FB), BF), vm((2, TH, 2048), BF), vm((2, TH, 2048), BF),
         vm((8, T), F32), vm((16, 8, T), F32), vm((8, T), F32), vm((8, 8, T), F32), vm((2, TH, FB), F32),
         vm((NG, TH, HALF), BF), vm((NG, TH, HALF), BF),
-        vm((NG, 3, 2 * TR, HALF), BF), vm((NG, 4, TR, HALF), BF),
-        vm((NG, TR, HALF), BF), vm((NG, TR, HALF), BF), vm((NG, 3, TR, HALF), BF), vm((NG, 3, TR, HALF), BF),
+        vm((NG, 2, 2 * TR, HALF), BF), vm((NG, 2, TR, HALF), BF), vm((NG, 2, TR, HALF), BF), vm((NG, 4, TR, HALF), BF),
+        vm((NG, TR, HALF), BF), vm((NG, TR, HALF), BF), vm((NG, TR, HALF), BF), vm((NG, 2, TR // 2, HALF), BF),
+        vm((NG, 2, TR // 2, HALF), BF), vm((NG, 2, TR // 2, HALF), BF), vm((NG, 2, TR, HALF), BF),
         vm((2, TR, V), F32), vm((FB, FB), F32), vm((2, 8, FB), F32), vm((2, 16, 8, FB), F32),
         vm((2, 8, TR, FB), F32), vm((2, TH, V), BF),
         dma((4,)), dma((8,)),
     ]
     counts = [
         (7, 2), (2, 4), (2, 8), (2, 4), (2, 8), (2, 8), (2, 8), (2, 8), (2, 8), (15,), (7,), (2, 15), (2, 7),
-        (NG, 3), (NG, 4), (NG,), (NG, 3),
-        (NG, 3), (NG,), (NG, 3), (NG, 3), (NG, 3), (NG,),
+        (NG, 2), (NG, 2), (NG, 2), (NG, 4), (NG,), (NG, 2), (NG, 2), (NG, 2),
+        (NG, 2), (NG, 2), (NG,), (NG, 3), (NG, 2), (NG, 2), (NG,), (NG, 2), (NG, 2),
     ]
     for n in counts:
         scratch += [dma(n), dma(n)]

time: 180 us -> 164 us (0.911)
  Pallas kernels: 177 us -> 160 us
    pallas_call x1, Pallas kernels: 173 us -> 156 us  [head(): pl.pallas_call(head_kernel, name='head', out_shape=(jax.ShapeDtypeStruct(...]
where the time goes in v5:
time: 164 us; the launch traced here: 163 us
  Pallas kernels  160 us (98%)
  between operations  2.38 us (1%)
    pallas_call x1, Pallas kernels, head(): pl.pallas_call(head_kernel, name='head', out_shape=(jax.ShapeDtypeStruct(...  156 us
    pallas_call x1, Pallas kernels, in_order(): pl.pallas_call(order_kernel, name='in_order', grid=(1024 // rows,), out_s...  4.21 us

profile of v5, /device:TPU:1, one launch (start us, length us, event | category | flops | bytes accessed | tf_op | source)
XLA Modules:
  0.0 162.7 jit_solution(6839122741579541435)
XLA Ops:
  0.6 156.1 %head.1 = (bf16[1024,2048]{1,0:T(8,128)(2,1)}, f32[1,1]{1,0:T(1,128)}) custom-call(bf16[64,1024]{1,0:T(8,128)(2,1)} %hid_ref.1, bf16[1024,16,128]{2,1,0:T(8,128)(2,1)} %bitcast.9, f32[1,128]{1,0:T(1,128)} %bitcast.12, bf16[4096,16,128]{2,1,0:T(8,128)(2,1)} %bitcast.8, s32[1,512]{1,0:T(1,128)} %bitcast.11), custom_call_target="tpu_custom_call" | custom-call | tf_op jit(solution)/shard_map/head/pallas_call | solution.py:763
  156.8 4.2 %in_order.1 = bf16[1024,16,128]{2,1,0:T(8,128)(2,1)} custom-call(bf16[1024,2048]{1,0:T(8,128)(2,1)} %get-tuple-element.4.grad), custom_call_target="tpu_custom_call" | custom-call | tf_op jit(solution)/shard_map/in_order/pallas_call | solution.py:783

commit v6 on v5

--- a/solution.py
+++ b/solution.py
@@ -12,7 +12,8 @@
 TH = T // 2
 TR = 32
 CH = 2048
-HALF = 1024
+ZW = 768
+XW = CH - ZW
 NG = 4
 ROWS = 256
 CODE = 32000.0
@@ -141,25 +142,25 @@
                 tcol[h, at : at + TR, :] = part[first : first + TR, :]
 
     def zcol(i):
-        return pl.ds(pl.multiple_of(i * CH, CH), HALF)
+        return pl.ds(pl.multiple_of(i * CH, CH), ZW)
 
     def xcol(i):
-        return pl.ds(pl.multiple_of(i * CH + HALF, HALF), HALF)
+        return pl.ds(pl.multiple_of(i * CH + ZW, FB), XW)
 
     for h in (0, 1):
         for i in (0, 1):
-            ids = (lax.broadcasted_iota(jnp.int32, (TH, HALF), 1) + i * CH).astype(F32)
+            ids = (lax.broadcasted_iota(jnp.int32, (TH, CH), 1) + i * CH).astype(F32)
             want = tcol[h, :, :1]
-            lz[h * 2 + i] = (ids == want).astype(BF)
-            lx[h * 2 + i] = (ids + HALF == want).astype(BF)
+            lz[h * 2 + i] = (ids[:, :ZW] == want).astype(BF)
+            lx[h * 2 + i] = (ids[:, ZW:] == want).astype(BF)
 
     def pick_body(n, carry):
         col = pl.ds(pl.multiple_of(n * 256, 256), 256)
         for h in (0, 1):
             r = jnp.zeros((TH, 256), F32)
             for i in (0, 1):
-                r = r + dot(lz[h * 2 + i], e_flat[i * CH : i * CH + HALF, col], NN)
-                r = r + dot(lx[h * 2 + i], e_flat[i * CH + HALF : (i + 1) * CH, col], NN)
+                r = r + dot(lz[h * 2 + i], e_flat[i * CH : i * CH + ZW, col], NN)
+                r = r + dot(lx[h * 2 + i], e_flat[i * CH + ZW : (i + 1) * CH, col], NN)
             oh[h, :, col] = r.astype(BF)
         return carry
 
@@ -343,12 +344,12 @@
 
     def logits_chunk(g):
         h, i = g // 2, g % 2
-        lx[g] = dot(nf[h], e_flat[i * CH + HALF : (i + 1) * CH, :], NT).astype(BF)
+        lx[g] = dot(nf[h], e_flat[i * CH + ZW : (i + 1) * CH, :], NT).astype(BF)
         for k in (0, 1):
             rxf_copy(g, k).start()
         for k in (0, 1):
             rxn_copy(g, k).start()
-        lz[g] = dot(nf[h], e_flat[i * CH : i * CH + HALF, :], NT).astype(BF)
+        lz[g] = dot(nf[h], e_flat[i * CH : i * CH + ZW, :], NT).astype(BF)
         for d in (2, 1, 3, 0):
             rz_copy(g, d).start()
 
@@ -461,16 +462,17 @@
         inv_own = inv_s[h, tok(pos), :][:, :1]
         want = tcol[h, tok(pos), :][:, :1]
         m = jnp.full((TR, 1), -jnp.inf, F32)
-        for j in range(V // HALF):
-            v = lg[h, :, j * HALF : (j + 1) * HALF] * inv_own
-            lg[h, :, j * HALF : (j + 1) * HALF] = v
+        spans = [(0, ZW), (ZW, XW), (CH, ZW), (CH + ZW, XW)]
+        for at, wide in spans:
+            v = lg[h, :, at : at + wide] * inv_own
+            lg[h, :, at : at + wide] = v
             m = jnp.maximum(m, jnp.max(v, axis=1, keepdims=True))
         s, sl, pk = (jnp.zeros((TR, 1), F32) for _ in range(3))
-        for j in range(V // HALF):
-            ids = (lax.broadcasted_iota(jnp.int32, (TR, HALF), 1) + j * HALF).astype(F32)
-            v = lg[h, :, j * HALF : (j + 1) * HALF]
+        for j, (at, wide) in enumerate(spans):
+            ids = (lax.broadcasted_iota(jnp.int32, (TR, wide), 1) + at).astype(F32)
+            v = lg[h, :, at : at + wide]
             p = jnp.exp(v - m)
-            dl[h, tok(pos), j * HALF : (j + 1) * HALF] = p.astype(BF)
+            dl[h, tok(pos), at : at + wide] = p.astype(BF)
             g = h * 2 + j // 2
             if j % 2:
                 axz_copy(g).start()
@@ -640,24 +642,24 @@
     statistics(0)
     ag_end(0)
     ag_end(1)
+    forward(2)
     factors(0)
     product(0, whole_tile(0), core2_ss, core2_rs, 1)
-    forward(2)
     forward(3)
+    forward_far(2)
     product(0, whole_tile(0), core2_ss, core2_rs, 0)
-    forward_far(2)
+    forward_far(3)
     exchange(0, core2_ss, core2_rs, mp2_ss, mp2_rs, GRAD_BOUND)
-    forward_far(3)
     statistics(1)
-    pre_gradient(0)
     ag_end(2)
     early_part(1)
+    pre_gradient(0)
     factors(1)
     ag_end(3)
     product(1, late_tile(1), core2_ss, core2_rs, 1)
-    gather_mid(dpf, 0, *dp_sems)
     product(1, late_tile(1), core2_ss, core2_rs, 0)
     exchange(1, core2_ss, core2_rs, mp2_ss, mp2_rs, GRAD_BOUND)
+    gather_mid(dpf, 0, *dp_sems)
     for h in (0, 1):
         for i in range(8):
             hid_t[i * FB : (i + 1) * FB, h * TH : (h + 1) * TH] = hid_all[h, :, i * FB : (i + 1) * FB].T
@@ -743,10 +745,10 @@
         vm((2, 8, TH, FB), jnp.int16), vm((2, TH, 2048), BF), vm((2, TH, FB), F32), vm((2, TH, FB), F32),
         vm((2, TH, FB), F32), vm((2, TH, FB), F32), vm((2, TH, FB), BF), vm((2, TH, 2048), BF), vm((2, TH, 2048), BF),
         vm((8, T), F32), vm((16, 8, T), F32), vm((8, T), F32), vm((8, 8, T), F32), vm((2, TH, FB), F32),
-        vm((NG, TH, HALF), BF), vm((NG, TH, HALF), BF),
-        vm((NG, 2, 2 * TR, HALF), BF), vm((NG, 2, TR, HALF), BF), vm((NG, 2, TR, HALF), BF), vm((NG, 4, TR, HALF), BF),
-        vm((NG, TR, HALF), BF), vm((NG, TR, HALF), BF), vm((NG, TR, HALF), BF), vm((NG, 2, TR // 2, HALF), BF),
-        vm((NG, 2, TR // 2, HALF), BF), vm((NG, 2, TR // 2, HALF), BF), vm((NG, 2, TR, HALF), BF),
+        vm((NG, TH, ZW), BF), vm((NG, TH, XW), BF),
+        vm((NG, 2, 2 * TR, XW), BF), vm((NG, 2, TR, XW), BF), vm((NG, 2, TR, XW), BF), vm((NG, 4, TR, ZW), BF),
+        vm((NG, TR, XW), BF), vm((NG, TR, XW), BF), vm((NG, TR, ZW), BF), vm((NG, 2, TR // 2, ZW), BF),
+        vm((NG, 2, TR // 2, ZW), BF), vm((NG, 2, TR // 2, ZW), BF), vm((NG, 2, TR, ZW), BF),
         vm((2, TR, V), F32), vm((FB, FB), F32), vm((2, 8, FB), F32), vm((2, 16, 8, FB), F32),
         vm((2, 8, TR, FB), F32), vm((2, TH, V), BF),
         dma((4,)), dma((8,)),

time: 164 us -> 159 us (0.970)
  Pallas kernels: 160 us -> 156 us
    pallas_call x1, Pallas kernels: 156 us -> 151 us  [head(): pl.pallas_call(head_kernel, name='head', out_shape=(jax.ShapeDtypeStruct(...]
where the time goes in v6:
time: 159 us; the launch traced here: 158 us
  Pallas kernels  156 us (98%)
  between operations  2.38 us (1%)
    pallas_call x1, Pallas kernels, head(): pl.pallas_call(head_kernel, name='head', out_shape=(jax.ShapeDtypeStruct(...  151 us
    pallas_call x1, Pallas kernels, in_order(): pl.pallas_call(order_kernel, name='in_order', grid=(1024 // rows,), out_s...  4.21 us

profile of v6, /device:TPU:1, one launch (start us, length us, event | category | flops | bytes accessed | tf_op | source)
XLA Modules:
  0.0 158.0 jit_solution(14189674761578777886)
XLA Ops:
  0.6 151.4 %head.1 = (bf16[1024,2048]{1,0:T(8,128)(2,1)}, f32[1,1]{1,0:T(1,128)}) custom-call(bf16[64,1024]{1,0:T(8,128)(2,1)} %hid_ref.1, bf16[1024,16,128]{2,1,0:T(8,128)(2,1)} %bitcast.9, f32[1,128]{1,0:T(1,128)} %bitcast.12, bf16[4096,16,128]{2,1,0:T(8,128)(2,1)} %bitcast.8, s32[1,512]{1,0:T(1,128)} %bitcast.11), custom_call_target="tpu_custom_call" | custom-call | tf_op jit(solution)/shard_map/head/pallas_call | solution.py:765
  152.1 4.2 %in_order.1 = bf16[1024,16,128]{2,1,0:T(8,128)(2,1)} custom-call(bf16[1024,2048]{1,0:T(8,128)(2,1)} %get-tuple-element.4.grad), custom_call_target="tpu_custom_call" | custom-call | tf_op jit(solution)/shard_map/in_order/pallas_call | solution.py:785

commit v7 on v6

--- a/solution.py
+++ b/solution.py
@@ -659,7 +659,6 @@
     product(1, late_tile(1), core2_ss, core2_rs, 1)
     product(1, late_tile(1), core2_ss, core2_rs, 0)
     exchange(1, core2_ss, core2_rs, mp2_ss, mp2_rs, GRAD_BOUND)
-    gather_mid(dpf, 0, *dp_sems)
     for h in (0, 1):
         for i in range(8):
             hid_t[i * FB : (i + 1) * FB, h * TH : (h + 1) * TH] = hid_all[h, :, i * FB : (i + 1) * FB].T
@@ -668,8 +667,9 @@
         for b in range(8):
             loss = loss + sc_all[h, b][:, 2:3]
     loss_ref[...] = jnp.sum(loss, axis=0, keepdims=True) / T
+    gather_mid(dpf, 0, *dp_sems)
+    pre_gradient(1)
     gather_end(dpf, 0, *dp_sems)
-    pre_gradient(1)
 
     def grad_copy(n, col):
         return pltpu.make_async_copy(w_flat.at[:, col], grad_ref.at[:, col], out_sem.at[n])

time: 159 us -> 159 us (level)
  no operation moved by 1% of the time
where the time goes in v7:
time: 159 us; the launch traced here: 158 us
  Pallas kernels  156 us (98%)
  between operations  2.38 us (1%)
    pallas_call x1, Pallas kernels, head(): pl.pallas_call(head_kernel, name='head', out_shape=(jax.ShapeDtypeStruct(...  151 us
    pallas_call x1, Pallas kernels, in_order(): pl.pallas_call(order_kernel, name='in_order', grid=(1024 // rows,), out_s...  4.21 us

profile of v7, /device:TPU:1, one launch (start us, length us, event | category | flops | bytes accessed | tf_op | source)
XLA Modules:
  0.0 158.0 jit_solution(11350900173718659742)
XLA Ops:
  0.6 151.4 %head.1 = (bf16[1024,2048]{1,0:T(8,128)(2,1)}, f32[1,1]{1,0:T(1,128)}) custom-call(bf16[64,1024]{1,0:T(8,128)(2,1)} %hid_ref.1, bf16[1024,16,128]{2,1,0:T(8,128)(2,1)} %bitcast.9, f32[1,128]{1,0:T(1,128)} %bitcast.12, bf16[4096,16,128]{2,1,0:T(8,128)(2,1)} %bitcast.8, s32[1,512]{1,0:T(1,128)} %bitcast.11), custom_call_target="tpu_custom_call" | custom-call | tf_op jit(solution)/shard_map/head/pallas_call | solution.py:765
  152.1 4.2 %in_order.1 = bf16[1024,16,128]{2,1,0:T(8,128)(2,1)} custom-call(bf16[1024,2048]{1,0:T(8,128)(2,1)} %get-tuple-element.4.grad), custom_call_target="tpu_custom_call" | custom-call | tf_op jit(solution)/shard_map/in_order/pallas_call | solution.py:785
